TPU v7x, 32 devices: a whole 2x2x4 slice. The times are simulated.
32 devices in a mesh: dp: 8 (over z, x), seq: 4 (over y, core).
Axes of the slice: x: 2, y: 2, z: 4, core: 2. Of those that a mesh axis runs over, the one named last changes fastest.
Arguments:
- tokens: bfloat16 [32, 1024, 768], P('dp', 'seq'), may hold values from -6 to 6
- cotangent: bfloat16 [32, 1024, 768], P('dp', 'seq'), may hold values from -6 to 6
- lengths: int32 [32], P('dp'), may hold values from 1 to 1024, as said below
- qkv_weight: float32 [768, 2304], P('dp'), may hold values from -0.21875 to 0.21875
- qkv_first: float32 [768, 2304], P('dp'), may hold values from -0.00390625 to 0.00390625
- qkv_second: float32 [768, 2304], P('dp'), may hold values from 5.4253474e-07 to 2.170139e-06
- qkv_average: float32 [768, 2304], P('dp'), may hold values from -0.21875 to 0.21875
- proj_weight: float32 [768, 768], P('dp'), may hold values from -1.75 to 1.75
- proj_first: float32 [768, 768], P('dp'), may hold values from -0.00048828125 to 0.00048828125
- proj_second: float32 [768, 768], P('dp'), may hold values from 6.781684e-09 to 2.7126736e-08
- proj_average: float32 [768, 768], P('dp'), may hold values from -1.75 to 1.75
- inner_weight: float32 [768, 3072], P('dp'), may hold values from -0.21875 to 0.21875
- inner_first: float32 [768, 3072], P('dp'), may hold values from -0.0004272461 to 0.0004272461
- inner_second: float32 [768, 3072], P('dp'), may hold values from 5.086263e-09 to 2.0345052e-08
- inner_average: float32 [768, 3072], P('dp'), may hold values from -0.21875 to 0.21875
- outer_weight: float32 [3072, 768], P('dp'), may hold values from -0.109375 to 0.109375
- outer_first: float32 [3072, 768], P('dp'), may hold values from -0.0007324219 to 0.0007324219
- outer_second: float32 [3072, 768], P('dp'), may hold values from 1.2715658e-08 to 5.086263e-08
- outer_average: float32 [3072, 768], P('dp'), may hold values from -0.109375 to 0.109375
- gains: float32 [2, 768], P(None, 'dp'), may hold values from 0.3 to 2.4
- gain_first: float32 [2, 768], P(None, 'dp'), may hold values from -0.009765625 to 0.009765625
- gain_second: float32 [2, 768], P(None, 'dp'), may hold values from 2.2605614e-06 to 9.042245e-06
- gain_average: float32 [2, 768], P(None, 'dp'), may hold values from 0.1 to 1.9
- mixes: float32 [2, 12, 12], replicated, may hold values from -0.9 to 1.3
- mix_first: float32 [2, 12, 12], replicated, may hold values from -0.01953125 to 0.01953125
- mix_second: float32 [2, 12, 12], replicated, may hold values from 9.042245e-06 to 3.616898e-05
- mix_average: float32 [2, 12, 12], replicated, may hold values from -0.4 to 1.2
Outputs:
- output: bfloat16 [32, 1024, 768], P('dp', 'seq')
- grad_tokens: float32 [32, 1024, 768], P('dp', 'seq')
- grad_norm: float32 [], replicated
- next_qkv_first: float32 [768, 2304], P('dp')
- next_qkv_second: float32 [768, 2304], P('dp')
- next_qkv_weight: float32 [768, 2304], P('dp')
- next_qkv_average: float32 [768, 2304], P('dp')
- next_proj_first: float32 [768, 768], P('dp')
- next_proj_second: float32 [768, 768], P('dp')
- next_proj_weight: float32 [768, 768], P('dp')
- next_proj_average: float32 [768, 768], P('dp')
- next_inner_first: float32 [768, 3072], P('dp')
- next_inner_second: float32 [768, 3072], P('dp')
- next_inner_weight: float32 [768, 3072], P('dp')
- next_inner_average: float32 [768, 3072], P('dp')
- next_outer_first: float32 [3072, 768], P('dp')
- next_outer_second: float32 [3072, 768], P('dp')
- next_outer_weight: float32 [3072, 768], P('dp')
- next_outer_average: float32 [3072, 768], P('dp')
- next_gain_first: float32 [2, 768], P(None, 'dp')
- next_gain_second: float32 [2, 768], P(None, 'dp')
- next_gains: float32 [2, 768], P(None, 'dp')
- next_gain_average: float32 [2, 768], P(None, 'dp')
- next_mix_first: float32 [2, 12, 12], replicated
- next_mix_second: float32 [2, 12, 12], replicated
- next_mixes: float32 [2, 12, 12], replicated
- next_mix_average: float32 [2, 12, 12], replicated
- clipped_gain_grad: float32 [2, 768], P(None, 'dp')
Inputs may be any that keep to these rules, and one draw needn't show every extreme that they name: `lengths`: in each aligned block of 4 sequences (one index of dp) at least one sequence has length 1024.
All inputs are finite; a program needn't handle non-finite values.
Results may differ from a plain program's by a relative error of at most 0.014.
The roundings to bfloat16 on the way count: a program that leaves them out, or rounds other values in their place, can miss the bound.
Values may be sent and summed in bfloat16 or wider, within the bound.
No kernel may reach another device: no remote copies, remote signals or barrier semaphores. Data moves between devices by JAX's collectives and lax.ppermute only.
A program may use at most 384 MiB of HBM per device.

v0:
```python
from functools import partial
import math

import jax
import jax.numpy as jnp
from jax import lax
from jax.sharding import PartitionSpec as P

STEP = 10


NORM_EPS = 1e-06
BETA = 0.5
ADAM_EPS = 1e-08
DECAY = 0.01
EMA_KEEP = 0.8
CLIP = 1.0


def inverse_rms(values):
    return lax.rsqrt(jnp.mean(values * values, axis=-1, keepdims=True) + NORM_EPS)


def rms_backward(scale_inv, normed, grad_normed):
    return scale_inv * (
        grad_normed - normed * jnp.mean(normed * grad_normed, axis=-1, keepdims=True)
    )


def mix_heads(matrix, values):
    total = matrix[0][None, :, None, None] * values[:, 0:1].astype(jnp.float32)
    for head in range(1, matrix.shape[0]):
        total = total + matrix[head][None, :, None, None] * values[:, head : head + 1].astype(
            jnp.float32
        )
    return total


def masked_scores(rows_q, keys_all, mixes, seq_lengths, first_row, scaling):
    scores = (
        jnp.einsum("sqhe,skhe->shqk", rows_q, keys_all, preferred_element_type=jnp.float32)
        * scaling
    ).astype(jnp.bfloat16)
    mixed = mix_heads(mixes[0], scores)
    key_pos = jnp.arange(keys_all.shape[1], dtype=jnp.int32)
    query_pos = first_row + jnp.arange(rows_q.shape[1], dtype=jnp.int32)
    allowed = (key_pos[None, None, None, :] <= query_pos[None, None, :, None]) & (
        key_pos[None, None, None, :] < seq_lengths[:, None, None, None]
    )
    return (scores, jnp.where(allowed, mixed, -1e30), allowed)


def adamw(weight, first, second, average, grad, rate):
    first_new = BETA * first + (1.0 - BETA) * grad
    second_new = BETA * second + (1.0 - BETA) * grad * grad
    fix = 1.0 - BETA**STEP
    weight_new = weight - rate * (
        first_new / fix / (jnp.sqrt(second_new / fix) + ADAM_EPS) + DECAY * weight
    )
    average_new = EMA_KEEP * average + (1.0 - EMA_KEEP) * weight_new
    return (first_new, second_new, weight_new, average_new)


def on_device(
    tokens,
    cotangent,
    lengths,
    qkv_weight,
    qkv_first,
    qkv_second,
    qkv_average,
    proj_weight,
    proj_first,
    proj_second,
    proj_average,
    inner_weight,
    inner_first,
    inner_second,
    inner_average,
    outer_weight,
    outer_first,
    outer_second,
    outer_average,
    gains,
    gain_first,
    gain_second,
    gain_average,
    mixes,
    mix_first,
    mix_second,
    mix_average,
):
    bfloat = jnp.bfloat16
    single_sequence = jnp.float32
    group_seqs, shard_len, width = tokens.shape
    seq_count = lax.axis_size("seq")
    per_dev = group_seqs // seq_count
    full_len = shard_len * seq_count
    heads = mixes.shape[1]
    head_dim = width // heads
    scaling = 1.0 / math.sqrt(head_dim)
    block_rows = min(512, full_len)
    block_count = full_len // block_rows
    query_key_value_gathered, projection_gathered, inner_gathered, outer_gathered, gain_low = (
        lax.all_gather(qkv_weight.astype(bfloat), "dp", axis=0, tiled=True),
        lax.all_gather(proj_weight.astype(bfloat), "dp", axis=0, tiled=True),
        lax.all_gather(inner_weight.astype(bfloat), "dp", axis=0, tiled=True),
        lax.all_gather(outer_weight.astype(bfloat), "dp", axis=0, tiled=True),
        lax.all_gather(gains.astype(bfloat), "dp", axis=1, tiled=True),
    )
    gain_vals = gain_low.astype(single_sequence)
    my_lengths = lax.dynamic_slice_in_dim(lengths, lax.axis_index("seq") * per_dev, per_dev)
    row_tokens, row_cot = (tokens, cotangent)
    positions = lax.axis_index("seq") * shard_len + jnp.arange(shard_len, dtype=jnp.int32)
    input_rows = row_tokens.astype(single_sequence)
    scale_one = inverse_rms(input_rows)
    normed_one = input_rows * scale_one
    first_layer_input = (normed_one * gain_vals[0]).astype(bfloat)
    query_key_value_local = jnp.einsum(
        "tpw,we->tpe",
        first_layer_input,
        query_key_value_gathered,
        preferred_element_type=single_sequence,
    ).astype(bfloat)
    qkv_seq = lax.all_to_all(query_key_value_local, "seq", split_axis=0, concat_axis=1, tiled=True)
    shape_four = (per_dev, full_len, heads, head_dim)
    queries = qkv_seq[..., :width].reshape(shape_four)
    keys_all = qkv_seq[..., width : 2 * width].reshape(shape_four)
    values_all = qkv_seq[..., 2 * width :].reshape(shape_four)

    def forward_block(block_index):
        first_row = block_index * block_rows
        rows_q = lax.dynamic_slice_in_dim(queries, first_row, block_rows, 1)
        unused, mixed, allowed = masked_scores(
            rows_q, keys_all, mixes, my_lengths, first_row, scaling
        )
        peak = jnp.max(mixed, axis=-1, keepdims=True)
        shifted = jnp.exp(mixed - peak)
        denom = jnp.sum(shifted, axis=-1, keepdims=True)
        probs_low = (shifted / denom).astype(bfloat)
        weights_low = mix_heads(mixes[1], probs_low).astype(bfloat)
        attended_rows = jnp.einsum(
            "siqk,skie->sqie", weights_low, values_all, preferred_element_type=single_sequence
        ).astype(bfloat)
        return (attended_rows, peak + jnp.log(denom))

    attended_blocks, log_sums = lax.map(forward_block, jnp.arange(block_count, dtype=jnp.int32))
    attended_seq = jnp.moveaxis(attended_blocks, 0, 1).reshape(per_dev, full_len, width)
    attention_output = lax.all_to_all(attended_seq, "seq", split_axis=1, concat_axis=0, tiled=True)
    residual_stream = input_rows + jnp.einsum(
        "yto,oz->ytz", attention_output, projection_gathered, preferred_element_type=single_sequence
    )
    scale_two = inverse_rms(residual_stream)
    normed_two = residual_stream * scale_two
    second_layer_input = (normed_two * gain_vals[1]).astype(bfloat)
    hidden_state = jnp.einsum(
        "tpw,we->tpe", second_layer_input, inner_gathered, preferred_element_type=single_sequence
    )
    active, gelu_back = jax.vjp(partial(jax.nn.gelu, approximate=True), hidden_state)
    active_reduced = active.astype(bfloat)
    output_rows = (
        residual_stream
        + jnp.einsum(
            "mrx,xk->mrk", active_reduced, outer_gathered, preferred_element_type=single_sequence
        )
    ).astype(bfloat)
    live = positions[None, :] < lengths[:, None]
    output_gradient = jnp.where(live[:, :, None], row_cot, jnp.zeros_like(row_cot))
    outer_gradient = jnp.einsum(
        "hua,hut->at", active_reduced, output_gradient, preferred_element_type=single_sequence
    )
    active_gradient = jnp.einsum(
        "avw,qw->avq", output_gradient, outer_gathered, preferred_element_type=single_sequence
    )
    hidden_gradient = gelu_back(active_gradient)[0].astype(bfloat)
    inner_gradient = jnp.einsum(
        "rxc,rxk->ck", second_layer_input, hidden_gradient, preferred_element_type=single_sequence
    )
    second_layer_gradient = jnp.einsum(
        "tkr,yr->tky", hidden_gradient, inner_gathered, preferred_element_type=single_sequence
    )
    gain_two = jnp.sum(second_layer_gradient * normed_two, axis=(0, 1))
    grad_resid = output_gradient.astype(single_sequence) + rms_backward(
        scale_two, normed_two, second_layer_gradient * gain_vals[1]
    )
    residual_reduced = grad_resid.astype(bfloat)
    projection_gradient = jnp.einsum(
        "mry,mrc->yc", attention_output, residual_reduced, preferred_element_type=single_sequence
    )
    grad_attended = jnp.einsum(
        "rmn,un->rmu", residual_reduced, projection_gathered, preferred_element_type=single_sequence
    ).astype(bfloat)
    grad_seq = lax.all_to_all(
        grad_attended, "seq", split_axis=0, concat_axis=1, tiled=True
    ).reshape(shape_four)

    def backward_block(running, block_inputs):
        grad_keys, grad_values, grad_mix_pre, grad_mix_post = running
        block_index, log_sum = block_inputs
        first_row = block_index * block_rows
        rows_q = lax.dynamic_slice_in_dim(queries, first_row, block_rows, 1)
        rows_grad = lax.dynamic_slice_in_dim(grad_seq, first_row, block_rows, 1)
        scores, mixed, allowed = masked_scores(
            rows_q, keys_all, mixes, my_lengths, first_row, scaling
        )
        probs = jnp.where(allowed, jnp.exp(mixed - log_sum), 0.0)
        probs_low = probs.astype(bfloat)
        weights_low = mix_heads(mixes[1], probs_low).astype(bfloat)
        grad_weights = jnp.einsum(
            "sqie,skie->siqk", rows_grad, values_all, preferred_element_type=single_sequence
        ).astype(bfloat)
        grad_values = grad_values + jnp.einsum(
            "siqk,sqie->skie", weights_low, rows_grad, preferred_element_type=single_sequence
        )
        grad_mix_post = grad_mix_post + jnp.einsum(
            "sjqk,siqk->ji", probs_low, grad_weights, preferred_element_type=single_sequence
        )
        grad_probs = mix_heads(mixes[1].T, grad_weights)
        grad_mixed = (
            probs * (grad_probs - jnp.sum(probs * grad_probs, axis=-1, keepdims=True))
        ).astype(bfloat)
        grad_mix_pre = grad_mix_pre + jnp.einsum(
            "shqk,sjqk->hj", scores, grad_mixed, preferred_element_type=single_sequence
        )
        grad_scores = mix_heads(mixes[0].T, grad_mixed).astype(bfloat)
        grad_rows = (
            jnp.einsum(
                "shqk,skhe->sqhe", grad_scores, keys_all, preferred_element_type=single_sequence
            )
            * scaling
        )
        grad_keys = (
            grad_keys
            + jnp.einsum(
                "shqk,sqhe->skhe", grad_scores, rows_q, preferred_element_type=single_sequence
            )
            * scaling
        )
        return ((grad_keys, grad_values, grad_mix_pre, grad_mix_post), grad_rows)

    zeros_four = jnp.zeros(shape_four, single_sequence)
    zeros_mix = jnp.zeros((heads, heads), single_sequence)
    running_end, grad_query_blocks = lax.scan(
        backward_block,
        (zeros_four, zeros_four, zeros_mix, zeros_mix),
        (jnp.arange(block_count, dtype=jnp.int32), log_sums),
    )
    grad_keys, grad_values, grad_mix_pre, grad_mix_post = running_end
    grad_queries = jnp.moveaxis(grad_query_blocks, 0, 1).reshape(per_dev, full_len, width)
    grad_qkv_seq = jnp.concatenate(
        [
            grad_queries,
            grad_keys.reshape(per_dev, full_len, width),
            grad_values.reshape(per_dev, full_len, width),
        ],
        axis=-1,
    ).astype(bfloat)
    local_query_key_value_gradient = lax.all_to_all(
        grad_qkv_seq, "seq", split_axis=1, concat_axis=0, tiled=True
    )
    query_key_value_gradient = jnp.einsum(
        "rxc,rxk->ck",
        first_layer_input,
        local_query_key_value_gradient,
        preferred_element_type=single_sequence,
    )
    first_layer_gradient = jnp.einsum(
        "tkr,yr->tky",
        local_query_key_value_gradient,
        query_key_value_gathered,
        preferred_element_type=single_sequence,
    )
    gain_one = jnp.sum(first_layer_gradient * normed_one, axis=(0, 1))
    grad_rows_tokens = grad_resid + rms_backward(
        scale_one, normed_one, first_layer_gradient * gain_vals[0]
    )
    grad_gains = jnp.stack([gain_one, gain_two])
    grad_mixes = jnp.stack([grad_mix_pre, grad_mix_post])
    owned = (
        lax.psum_scatter(query_key_value_gradient, "dp", scatter_dimension=0, tiled=True),
        lax.psum_scatter(projection_gradient, "dp", scatter_dimension=0, tiled=True),
        lax.psum_scatter(inner_gradient, "dp", scatter_dimension=0, tiled=True),
        lax.psum_scatter(outer_gradient, "dp", scatter_dimension=0, tiled=True),
        lax.psum_scatter(grad_gains, "dp", scatter_dimension=1, tiled=True),
    )
    summed = lax.psum((owned[0], owned[1], owned[2], owned[3], owned[4], grad_mixes), "seq")
    red_qkv, red_proj, red_inner, red_outer, red_gains, partial_mix = summed
    local_squares = (
        jnp.sum(red_qkv * red_qkv)
        + jnp.sum(red_proj * red_proj)
        + jnp.sum(red_inner * red_inner)
        + jnp.sum(red_outer * red_outer)
        + jnp.sum(red_gains * red_gains)
    )
    total_squares, red_mixes = lax.psum((local_squares, partial_mix), "dp")
    grad_norm = jnp.sqrt(total_squares + jnp.sum(red_mixes * red_mixes))
    factor = CLIP / jnp.maximum(grad_norm, CLIP)
    clipped_gains = red_gains * factor
    qkv_new = adamw(qkv_weight, qkv_first, qkv_second, qkv_average, red_qkv * factor, 0.03)
    proj_new = adamw(proj_weight, proj_first, proj_second, proj_average, red_proj * factor, 0.1)
    inner_new = adamw(
        inner_weight, inner_first, inner_second, inner_average, red_inner * factor, 0.03
    )
    outer_new = adamw(
        outer_weight, outer_first, outer_second, outer_average, red_outer * factor, 0.02
    )
    gain_new = adamw(gains, gain_first, gain_second, gain_average, clipped_gains, 0.3)
    mix_new = adamw(mixes, mix_first, mix_second, mix_average, red_mixes * factor, 0.3)
    return (
        output_rows,
        grad_rows_tokens,
        grad_norm,
        qkv_new[0],
        qkv_new[1],
        qkv_new[2],
        qkv_new[3],
        proj_new[0],
        proj_new[1],
        proj_new[2],
        proj_new[3],
        inner_new[0],
        inner_new[1],
        inner_new[2],
        inner_new[3],
        outer_new[0],
        outer_new[1],
        outer_new[2],
        outer_new[3],
        gain_new[0],
        gain_new[1],
        gain_new[2],
        gain_new[3],
        mix_new[0],
        mix_new[1],
        mix_new[2],
        mix_new[3],
        clipped_gains,
    )


def solution(mesh):
    in_specs = (
        P("dp", "seq", None),
        P("dp", "seq", None),
        P("dp"),
        P("dp", None),
        P("dp", None),
        P("dp", None),
        P("dp", None),
        P("dp", None),
        P("dp", None),
        P("dp", None),
        P("dp", None),
        P("dp", None),
        P("dp", None),
        P("dp", None),
        P("dp", None),
        P("dp", None),
        P("dp", None),
        P("dp", None),
        P("dp", None),
        P(None, "dp"),
        P(None, "dp"),
        P(None, "dp"),
        P(None, "dp"),
        P(),
        P(),
        P(),
        P(),
    )
    out_specs = (
        P("dp", "seq", None),
        P("dp", "seq", None),
        P(),
        P("dp", None),
        P("dp", None),
        P("dp", None),
        P("dp", None),
        P("dp", None),
        P("dp", None),
        P("dp", None),
        P("dp", None),
        P("dp", None),
        P("dp", None),
        P("dp", None),
        P("dp", None),
        P("dp", None),
        P("dp", None),
        P("dp", None),
        P("dp", None),
        P(None, "dp"),
        P(None, "dp"),
        P(None, "dp"),
        P(None, "dp"),
        P(),
        P(),
        P(),
        P(),
        P(None, "dp"),
    )
    return jax.shard_map(
        on_device, mesh=mesh, in_specs=in_specs, out_specs=out_specs, check_vma=False
    )
```

profile of v0, /device:TPU:0, one launch (start us, length us, event | category | flops | bytes accessed | tf_op | source)
XLA Modules:
  0.0 1998.5 jit_solution(2895077085683750040)
XLA Ops:
  36.6 42.1 %all-gather.6.cloned.1.call-done = bf16[768,2304]{1,0:T(8,128)(2,1)} async-done(((bf16[96,2304]{1,0:T(8,128)(2,1)}), bf16[768,2304]{1,0:T(8,128)(2,1)}) %all-gather.6.cloned.1.call-update) | async-done | bytes 3538960 | tf_op jit(solution)/shard_map/all_gather | solution.py:105
  93.1 52.2 %all-to-all-done = bf16[4,256,2304]{2,1,0:T(8,128)(2,1)} async-done(((bf16[4,256,2304]{2,1,0:T(8,128)(2,1)}), bf16[4,256,2304]{2,1,0:T(8,128)(2,1)}, u32[]{:S(2)}, u32[]{:S(2)}) %all-to-all-start) | async-done | bytes 4718624 | tf_op jit(solution)/shard_map/all_to_all | solution.py:125
  155.0 197.1 %while.31 = (s32[]{:T(128)}, bf16[2,1,512,12,64]{2,4,3,1,0:T(8,128)(2,1)}, f32[2,1,12,512,1]{3,2,4,1,0:T(8,128)S(1)}, f32[2,12,12]{2,1,0:T(8,128)S(1)}, s32[2]{0...) while((s32[]{:T(128)}, ...), condition=%wide.region_4.5_spmd, body=%wide.region_1.4_spmd.sunk | while | flops 1976954368 | bytes 232490576 | solution.py:147
  218.8 30.4 %fusion.233 = bf16[2,1,512,12,64]{2,4,3,1,0:T(8,128)(2,1)} fusion(bf16[2,1,512,12,64]{2,4,3,1,0:T(8,128)(2,1)} %get-tuple-element.1127, s32[]{:T(128)S(6)} %copy.380, bf16[1,1024,12,64]{1,3,2,0:T(8,128)(2,1)} %get-tuple-element.1147, f32[512,1024]{1,0:T(8,128)} %get-tuple-element.975, f32[12]{0:T(128)S(1)} %get-tuple-element.976, ...), kind=kOutput, calls=%fused_computation.14.clone.1 | convolution fusion | flops 956694528 | bytes 27525700 | tf_op jit(solution)/shard_map/while/body/eval_jaxpr/siqk,skie->sqie/dot_general | solution.py:142
  312.5 30.3 %fusion.233 = bf16[2,1,512,12,64]{2,4,3,1,0:T(8,128)(2,1)} fusion(bf16[2,1,512,12,64]{2,4,3,1,0:T(8,128)(2,1)} %get-tuple-element.1127, s32[]{:T(128)S(6)} %copy.380, bf16[1,1024,12,64]{1,3,2,0:T(8,128)(2,1)} %get-tuple-element.1147, f32[512,1024]{1,0:T(8,128)} %get-tuple-element.975, f32[12]{0:T(128)S(1)} %get-tuple-element.976, ...), kind=kOutput, calls=%fused_computation.14.clone.1 | convolution fusion | flops 956694528 | bytes 27525700 | tf_op jit(solution)/shard_map/while/body/eval_jaxpr/siqk,skie->sqie/dot_general | solution.py:142
  505.5 976.5 %while.32 = (s32[]{:T(128)}, f32[1,1024,12,64]{1,3,2,0:T(8,128)}, f32[1,1024,12,64]{1,3,2,0:T(8,128)}, f32[12,12]{1,0:T(8,128)}, f32[12,12]{1,0:T(8,128)S(1)}, /...) while((s32[]{:T(128)}, f32[1,1024,12,64]{1,3,2,0:T(8,128)}, ...), condition=%wide.region_9.10_spmd.clone, body=%wide.region_7.9_spmd.clone.sunk | while | flops 5667680256 | bytes 801748864 | solution.py:243
  621.1 36.5 %fusion.253 = f32[12,12]{1,0:T(8,128)S(1)} fusion(bf16[12,512,1024]{1,0,2:T(8,128)(2,1)} %copy.373, f32[12,12]{1,0:T(8,128)S(1)} %get-tuple-element.1174, pred[]{:T(512)S(6)} %compare.3, f32[12,512]{1,0:T(8,128)S(1)} %dynamic-slice_bitcast_fusion.2, f32[512,1024]{0,1:T(8,128)} %copy.361, f32[12]{0:T(128)S(1)} %get-tuple-element.1014, ...), kind=kOutput, calls=%fused_computation.119.clone.2 | convolution fusion | flops 320864512 | bytes 38299328 | tf_op jit(solution)/shard_map/while/body/eval_jaxpr/sjqk,siqk->ji/dot_general | solution.py:215
  657.6 31.0 %fusion.248 = (bf16[1,12,512,1024]{3,2,1,0:T(8,128)(2,1)S(1)}, f32[1,12,512,1024]{3,2,1,0:T(8,128)}) fusion(f32[12,512]{1,0:T(8,128)S(1)} %dynamic-slice_bitcast_fusion.2, f32[512,1024]{1,0:T(8,128)S(1)} %copy-done.7, f32[12]{0:T(128)S(1)} %get-tuple-element.1014, f32[512,1024]{1,0:T(8,128)} %get-tuple-element.1015, f32[12]{0:T(128)S(1)} %get-tuple-element.1016, ...), kind=kLoop, calls=%fused_computation.391.clone.1 | loop fusion | flops 169869312 | bytes 63464000 | tf_op jit(solution)/shard_map/while/body/eval_jaxpr/convert_element_type | solution.py:207
  696.7 29.3 %bitcast_add_fusion.5 = f32[1,1024,12,64]{1,3,2,0:T(8,128)} fusion(f32[1,1024,12,64]{1,3,2,0:T(8,128)} %get-tuple-element.1172, f32[512,1024]{1,0:T(8,128)} %get-tuple-element.1089, f32[12]{0:T(128)S(1)} %copy-done.81, f32[512,1024]{1,0:T(8,128)} %get-tuple-element.1091, f32[12]{0:T(128)S(1)} %copy-done.82, f32[512,1024]{1,0:T(8,128)} %get-tuple-element.1093, ...), kind=kOutput, calls=%fused_computation.107.clone.1 | convolution fusion | flops 957874176 | bytes 32244292 | tf_op jit(solution)/shard_map/while/body/eval_jaxpr/siqk,sqie->skie/dot_general | solution.py:212
  738.4 31.3 %multiply_reduce_fusion.11 = f32[12,512]{1,0:T(8,128)S(1)} fusion(f32[1,12,512,1024]{3,2,1,0:T(8,128)} %get-tuple-element.1037, f32[512,1024]{1,0:T(8,128)S(1)} %get-tuple-element.1038, f32[12]{0:T(128)S(1)} %copy-done.52, f32[512,1024]{1,0:T(8,128)S(1)} %get-tuple-element.1041, f32[12]{0:T(128)S(1)} %copy-done.53, ...), kind=kLoop, calls=%fused_computation.98.clone.1 | loop fusion | flops 157280256 | bytes 50356800 | tf_op jit(solution)/shard_map/while/body/eval_jaxpr/reduce_sum | solution.py:220
  769.8 29.0 %multiply_convert_fusion.22 = bf16[1,12,512,1024]{3,2,1,0:T(8,128)(2,1)} fusion(f32[1,12,512,1024]{3,2,1,0:T(8,128)} %get-tuple-element.1037, f32[12,512]{1,0:T(8,128)S(1)} %multiply_reduce_fusion.11, f32[512,1024]{1,0:T(8,128)S(1)} %get-tuple-element.1038, f32[12]{0:T(128)S(1)} %copy-done.52, f32[512,1024]{1,0:T(8,128)S(1)} %get-tuple-element.1041, ...), kind=kLoop, calls=%fused_computation.97.clone.1 | loop fusion | flops 163577856 | bytes 62939712 | tf_op jit(solution)/shard_map/while/body/eval_jaxpr/convert_element_type | solution.py:221
  832.7 104.2 %fusion.252 = f32[12,12]{1,0:T(8,128)S(1)} fusion(bf16[12,512,1024]{1,0,2:T(8,128)(2,1)} %copy.348, f32[12,512]{1,0:T(8,128)S(1)} %multiply_reduce_fusion.11, f32[512,1024]{0,1:T(8,128)} %copy.349, f32[12]{0:T(128)S(1)} %copy-done.52, f32[512,1024]{0,1:T(8,128)} %copy.350, f32[12]{0:T(128)S(1)} %copy-done.53, f32[512,1024]{0,1:T(8,128)} %copy.351, ...), kind=kOutput, calls=%fused_computation.118.clone.2 | convolution fusion | flops 478150912 | bytes 63490304 | tf_op jit(solution)/shard_map/while/body/eval_jaxpr/shqk,sjqk->hj/dot_general | solution.py:222
  1105.3 36.2 %fusion.253 = f32[12,12]{1,0:T(8,128)S(1)} fusion(bf16[12,512,1024]{1,0,2:T(8,128)(2,1)} %copy.373, f32[12,12]{1,0:T(8,128)S(1)} %get-tuple-element.1174, pred[]{:T(512)S(6)} %compare.3, f32[12,512]{1,0:T(8,128)S(1)} %dynamic-slice_bitcast_fusion.2, f32[512,1024]{0,1:T(8,128)} %copy.361, f32[12]{0:T(128)S(1)} %get-tuple-element.1014, ...), kind=kOutput, calls=%fused_computation.119.clone.2 | convolution fusion | flops 320864512 | bytes 38299328 | tf_op jit(solution)/shard_map/while/body/eval_jaxpr/sjqk,siqk->ji/dot_general | solution.py:215
  1141.5 31.0 %fusion.248 = (bf16[1,12,512,1024]{3,2,1,0:T(8,128)(2,1)S(1)}, f32[1,12,512,1024]{3,2,1,0:T(8,128)}) fusion(f32[12,512]{1,0:T(8,128)S(1)} %dynamic-slice_bitcast_fusion.2, f32[512,1024]{1,0:T(8,128)S(1)} %copy-done.7, f32[12]{0:T(128)S(1)} %get-tuple-element.1014, f32[512,1024]{1,0:T(8,128)} %get-tuple-element.1015, f32[12]{0:T(128)S(1)} %get-tuple-element.1016, ...), kind=kLoop, calls=%fused_computation.391.clone.1 | loop fusion | flops 169869312 | bytes 63464000 | tf_op jit(solution)/shard_map/while/body/eval_jaxpr/convert_element_type | solution.py:207
  1180.6 29.0 %bitcast_add_fusion.5 = f32[1,1024,12,64]{1,3,2,0:T(8,128)} fusion(f32[1,1024,12,64]{1,3,2,0:T(8,128)} %get-tuple-element.1172, f32[512,1024]{1,0:T(8,128)} %get-tuple-element.1089, f32[12]{0:T(128)S(1)} %copy-done.81, f32[512,1024]{1,0:T(8,128)} %get-tuple-element.1091, f32[12]{0:T(128)S(1)} %copy-done.82, f32[512,1024]{1,0:T(8,128)} %get-tuple-element.1093, ...), kind=kOutput, calls=%fused_computation.107.clone.1 | convolution fusion | flops 957874176 | bytes 32244292 | tf_op jit(solution)/shard_map/while/body/eval_jaxpr/siqk,sqie->skie/dot_general | solution.py:212
  1221.9 30.9 %multiply_reduce_fusion.11 = f32[12,512]{1,0:T(8,128)S(1)} fusion(f32[1,12,512,1024]{3,2,1,0:T(8,128)} %get-tuple-element.1037, f32[512,1024]{1,0:T(8,128)S(1)} %get-tuple-element.1038, f32[12]{0:T(128)S(1)} %copy-done.52, f32[512,1024]{1,0:T(8,128)S(1)} %get-tuple-element.1041, f32[12]{0:T(128)S(1)} %copy-done.53, ...), kind=kLoop, calls=%fused_computation.98.clone.1 | loop fusion | flops 157280256 | bytes 50356800 | tf_op jit(solution)/shard_map/while/body/eval_jaxpr/reduce_sum | solution.py:220
  1252.9 28.6 %multiply_convert_fusion.22 = bf16[1,12,512,1024]{3,2,1,0:T(8,128)(2,1)} fusion(f32[1,12,512,1024]{3,2,1,0:T(8,128)} %get-tuple-element.1037, f32[12,512]{1,0:T(8,128)S(1)} %multiply_reduce_fusion.11, f32[512,1024]{1,0:T(8,128)S(1)} %get-tuple-element.1038, f32[12]{0:T(128)S(1)} %copy-done.52, f32[512,1024]{1,0:T(8,128)S(1)} %get-tuple-element.1041, ...), kind=kLoop, calls=%fused_computation.97.clone.1 | loop fusion | flops 163577856 | bytes 62939712 | tf_op jit(solution)/shard_map/while/body/eval_jaxpr/convert_element_type | solution.py:221
  1315.3 104.2 %fusion.252 = f32[12,12]{1,0:T(8,128)S(1)} fusion(bf16[12,512,1024]{1,0,2:T(8,128)(2,1)} %copy.348, f32[12,512]{1,0:T(8,128)S(1)} %multiply_reduce_fusion.11, f32[512,1024]{0,1:T(8,128)} %copy.349, f32[12]{0:T(128)S(1)} %copy-done.52, f32[512,1024]{0,1:T(8,128)} %copy.350, f32[12]{0:T(128)S(1)} %copy-done.53, f32[512,1024]{0,1:T(8,128)} %copy.351, ...), kind=kOutput, calls=%fused_computation.118.clone.2 | convolution fusion | flops 478150912 | bytes 63490304 | tf_op jit(solution)/shard_map/while/body/eval_jaxpr/shqk,sjqk->hj/dot_general | solution.py:222
  1516.3 49.0 %reduce.56 = bf16[1024,2304]{1,0:T(8,128)(2,1)} reduce(bf16[1024,1,2304]{2,1,0:T(2,128)(2,1)} %bitcast.711, bf16[]{:T(256)} %broadcast.2031), dimensions={1}, to_apply=%bitcast.604.reduce_sub_computation | reduce | bytes 9437186
  1570.7 59.8 %all_to_all.45 = bf16[4,2,294912]{2,1,0:T(2,128)(2,1)} all-to-all(bf16[4,2,294912]{2,1,0:T(2,128)(2,1)} %reshape.1506), channel_id=1, replica_groups=mesh['dp'=8,'seq'=4] {'seq'}, dimensions={0} | all-to-all | bytes 9437184 | tf_op jit(solution)/shard_map/all_to_all | solution.py:258
  1663.1 115.5 %reduce-scatter.8.cloned.1.call-done = f32[96,2304]{1,0:T(8,128)} async-done(((f32[768,2304]{1,0:T(8,128)}), f32[96,2304]{1,0:T(8,128)}) %reduce-scatter.8.cloned.1.call-update) | async-done | bytes 884752 | tf_op jit(solution)/shard_map/reduce_scatter | solution.py:280
  1793.9 49.3 %reduce-scatter.16.cloned.1.call-done = f32[96,2]{1,0:T(8,128)} async-done(((f32[768,2]{1,0:T(8,128)}), f32[96,2]{1,0:T(8,128)}) %reduce-scatter.16.cloned.1.call-update) | async-done | bytes 784
  1856.0 64.4 %all-reduce.5.cloned.1.call-done = (f32[96,2304]{1,0:T(8,128)}, f32[96,768]{1,0:T(8,128)}, f32[96,3072]{1,0:T(8,128)}, f32[384,768]{1,0:T(8,128)}) async-done(((f32[96,2304]{1,0:T(8,128)}, f32[96,768]{1,0:T(8,128)}, f32[96,3072]{1,0:T(8,128)}, f32[384,768]{1,0:T(8,128)}), (f32[96,2304]{1,0:T(8,128)}, f32[96,768]{1,0:T(8,128)}, f32[96,3072]{1,0:T(8,128)}, f32[384,768]{1,0:T(8,128)})) %all-reduce.5.cloned.1.call-update) | async-done | bytes 3538960 | tf_op jit(solution)/shard_map/psum | solution.py:286
  1931.7 38.0 %all-reduce = (f32[]{:T(128)}, f32[2,12,12]{2,1,0:T(8,128)S(1)}) all-reduce(f32[]{:T(128)S(6)} %add.1140, f32[2,12,12]{2,1,0:T(8,128)} %get-tuple-element.510), channel_id=1, replica_groups=mesh['dp'=8,'seq'=4] {'dp'}, use_global_device_ids=true, to_apply=%region_28.29 | all-reduce | flops 289 | bytes 2312 | tf_op jit(solution)/shard_map/psum | solution.py:295
  (560 shorter events, 902.7 us)
Async XLA Ops:
  7.2 71.5 %all-gather.6.cloned.1.call-start = ((), (), s32[]{:S(2)}) async-start(), calls=%async_computation.9 | async-start | bytes 3981312 | tf_op jit(solution)/shard_map/all_gather | solution.py:105
  9.4 400.0 %all-gather.8.cloned.1.call-start = ((), (), s32[]{:S(2)}) async-start(), calls=%async_computation.10 | async-start | bytes 1327104 | tf_op jit(solution)/shard_map/all_gather | solution.py:106
  11.1 402.1 %all-gather.10.cloned.1.call-start = ((), (), s32[]{:S(2)}) async-start(), calls=%async_computation.11 | async-start | bytes 5308416 | tf_op jit(solution)/shard_map/all_gather | solution.py:107
  36.2 50.1 %copy-start.76 = (f32[768]{0:T(1024)}, f32[768]{0:T(1024)S(1)}, u32[]{:S(2)}) copy-start(f32[768]{0:T(1024)S(1)} %get-tuple-element.460) | copy-start | bytes 9220
  36.6 49.7 %copy-start.78 = (f32[4,256]{1,0:T(4,128)}, f32[4,256]{1,0:T(4,128)S(1)}, u32[]{:S(2)}) copy-start(f32[4,256]{1,0:T(4,128)S(1)} %add_rsqrt_fusion.1) | copy-start | bytes 12292
  86.4 59.0 %all-to-all-start = ((bf16[4,256,2304]{2,1,0:T(8,128)(2,1)}), bf16[4,256,2304]{2,1,0:T(8,128)(2,1)}, u32[]{:S(2)}, u32[]{:S(2)}) async-start(bf16[4,256,2304]{2,1,0:T(8,128)(2,1)} %convolution_convert_fusion.1), calls=%async_computation | async-start | bytes 9437184 | tf_op jit(solution)/shard_map/all_to_all | solution.py:125
  91.5 333.2 %all-gather.12.cloned.1.call-start = ((), (), s32[]{:S(2)}) async-start(), calls=%async_computation.12 | async-start | bytes 5308416 | tf_op jit(solution)/shard_map/all_gather | solution.py:108
  380.3 24.5 %all-to-all-start.1 = ((bf16[4,2,98304]{2,1,0:T(2,128)(2,1)}), bf16[4,2,98304]{2,1,0:T(2,128)(2,1)}, u32[]{:S(2)}, u32[]{:S(2)}) async-start(bf16[4,2,98304]{2,1,0:T(2,128)(2,1)} %reshape.1504), calls=%async_computation.1 | async-start | bytes 3145728 | tf_op jit(solution)/shard_map/all_to_all | solution.py:149
  384.6 1278.4 %reduce-scatter.10.cloned.1.call-start = ((), (), s32[]{:S(2)}) async-start(), calls=%async_computation.14 | async-start | bytes 2654208 | tf_op jit(solution)/shard_map/reduce_scatter | solution.py:281
  456.3 1206.7 %reduce-scatter.14.cloned.1.call-start = ((), (), s32[]{:S(2)}) async-start(), calls=%async_computation.16 | async-start | bytes 10616832 | tf_op jit(solution)/shard_map/reduce_scatter | solution.py:283
  473.4 24.5 %all-to-all-start.2 = ((bf16[4,256,768]{2,1,0:T(8,128)(2,1)}), bf16[4,256,768]{2,1,0:T(8,128)(2,1)}, u32[]{:S(2)}, u32[]{:S(2)}) async-start(bf16[4,256,768]{2,1,0:T(8,128)(2,1)} %convolution_convert_fusion.2), calls=%async_computation.2 | async-start | bytes 3145728 | tf_op jit(solution)/shard_map/all_to_all | solution.py:193
  477.8 1185.3 %reduce-scatter.12.cloned.1.call-start = ((), (), s32[]{:S(2)}) async-start(), calls=%async_computation.15 | async-start | bytes 10616832 | tf_op jit(solution)/shard_map/reduce_scatter | solution.py:282
  488.5 1290.1 %reduce-scatter.8.cloned.1.call-start = ((), (), s32[]{:S(2)}) async-start(), calls=%async_computation.13 | async-start | bytes 7962624 | tf_op jit(solution)/shard_map/reduce_scatter | solution.py:280
  621.1 36.5 %copy-start.7 = (f32[512,1024]{1,0:T(8,128)S(1)}, f32[512,1024]{1,0:T(8,128)}, u32[]{:S(2)}) copy-start(f32[512,1024]{1,0:T(8,128)} %get-tuple-element.1013) | copy-start | bytes 6291460 | tf_op jit(solution)/shard_map/while
  621.1 36.5 %copy-start.13 = (pred[512,1024]{1,0:T(8,128)(4,1)S(1)}, pred[512,1024]{1,0:T(8,128)(4,1)}, u32[]{:S(2)}) copy-start(pred[512,1024]{1,0:T(8,128)(4,1)} %copy.347) | copy-start | bytes 1572868 | tf_op jit(solution)/shard_map/while
  1651.6 191.7 %reduce-scatter.16.cloned.1.call-start = ((), (), s32[]{:S(2)}) async-start(), calls=%async_computation.17 | async-start | bytes 442368
  1652.2 126.4 %copy-start.18 = (f32[4,256,768]{2,1,0:T(8,128)S(1)}, f32[4,256,768]{2,1,0:T(8,128)}, u32[]{:S(2)}) copy-start(f32[4,256,768]{2,1,0:T(8,128)} %copy-done.17) | copy-start | bytes 9437188
  1662.9 257.5 %all-reduce.5.cloned.1.call-start = ((), (), s32[]{:S(2)}) async-start(), calls=%async_computation.18 | async-start | bytes 7077888 | tf_op jit(solution)/shard_map/psum | solution.py:286
  1791.4 184.9 %copy-start.38 = (f32[96,768]{1,0:T(8,128)S(1)}, f32[96,768]{1,0:T(8,128)}, u32[]{:S(2)}) copy-start(f32[96,768]{1,0:T(8,128)} %param.38) | copy-start | bytes 884740
  1791.4 184.9 %copy-start.49 = (f32[96,768]{1,0:T(8,128)S(1)}, f32[96,768]{1,0:T(8,128)}, u32[]{:S(2)}) copy-start(f32[96,768]{1,0:T(8,128)} %param.41) | copy-start | bytes 884740
  1791.4 184.9 %copy-start.50 = (f32[96,768]{1,0:T(8,128)S(1)}, f32[96,768]{1,0:T(8,128)}, u32[]{:S(2)}) copy-start(f32[96,768]{1,0:T(8,128)} %param.40) | copy-start | bytes 884740
  1793.9 184.9 %copy-start.31 = (f32[96,2304]{1,0:T(8,128)S(1)}, f32[96,2304]{1,0:T(8,128)}, u32[]{:S(2)}) copy-start(f32[96,2304]{1,0:T(8,128)} %param.34) | copy-start | bytes 2654212
  1793.9 184.9 %copy-start.45 = (f32[96,2304]{1,0:T(8,128)S(1)}, f32[96,2304]{1,0:T(8,128)}, u32[]{:S(2)}) copy-start(f32[96,2304]{1,0:T(8,128)} %param.37) | copy-start | bytes 2654212
  1920.4 58.4 %copy-start.30 = (f32[96,2304]{1,0:T(8,128)S(1)}, f32[96,2304]{1,0:T(8,128)}, u32[]{:S(2)}) copy-start(f32[96,2304]{1,0:T(8,128)} %get-tuple-element.511) | copy-start | bytes 2654212
  (151 other events, 1487.4 us)
Sparse Core Ops, SparseCore 0:
  10.8 67.8 all-gather.5
  81.5 39.5 all-gather.7
  123.9 78.6 all-gather.9
  205.2 78.0 all-gather.11
  456.4 66.7 reduce-scatter.9
  526.7 162.4 reduce-scatter.13
  692.8 162.5 reduce-scatter.11
  1651.7 126.8 reduce-scatter.7
  1782.8 60.4 reduce-scatter.15
  1845.9 74.4 all-reduce.4
where the time goes:
time: 2010 us; the launch traced here: 2000 us
  matrix products  588 us (29%)
  other arithmetic  522 us (26%)
  waiting for transfers between devices  353 us (18%)
  local copies, waits for them, and re-layouts  346 us (17%)
  blocking collectives  131 us (7%)
  loops' own time  22.3 us (1%)
  between operations  21.1 us (1%)
    dot_general x2, matrix products, backward_block(): jnp.einsum('shqk,sjqk->hj', scores, grad_mixed, preferred_element_type=si...  208 us
    mul x44, local copies, waits for them, and re-layouts, mix_heads(): matrix[head][None, :, None, None]  126 us
    reduce_scatter x1, waiting for transfers between devices, on_device(): lax.psum_scatter(query_key_value_gradient, 'dp', scatter_dimension=0, til...  116 us
    mul x12, other arithmetic, mix_heads(): total = matrix[0][None, :, None, None] * values[:, 0:1].astype(jnp.float32)  104 us
    dot_general x2, matrix products, backward_block(): jnp.einsum('sjqk,siqk->ji', probs_low, grad_weights, preferred_element_ty...  72.7 us
    psum x1, waiting for transfers between devices, on_device(): lax.psum((owned[0], owned[1], owned[2], owned[3], owned[4], grad_mixes),...  64.4 us
    reduce_sum x2, other arithmetic, backward_block(): jnp.sum(probs * grad_probs, axis=-1, keepdims=True)  62.2 us
    convert_element_type x2, other arithmetic, backward_block(): probs_low = probs.astype(bfloat)  61.9 us
  transfers between devices with their start and end apart: 13, of which 7 were waited for; matrix products, arithmetic and copies ran while one was open for 69% of the time, Pallas kernels for 0%

commit v1 on v0

v1 whole, which is shorter than its diff:
```python
from functools import partial
import math

import jax
import jax.numpy as jnp
from jax import lax
from jax.experimental import pallas as pl
from jax.experimental.pallas import tpu as pltpu
from jax.sharding import PartitionSpec as P

STEP = 10

NORM_EPS = 1e-06
BETA = 0.5
ADAM_EPS = 1e-08
DECAY = 0.01
EMA_KEEP = 0.8
CLIP = 1.0

BF = jnp.bfloat16
F32 = jnp.float32
ROWS = 128
KEYS = 256
GROUP = 16
LANES = 128
SIDE = {1: 4, 2: 4, 3: 2, 4: 2}
NT = (((1,), (1,)), ((), ()))
NN = (((1,), (0,)), ((), ()))
TN = (((0,), (0,)), ((), ()))


def dot(left, right, dims=NN):
    return lax.dot_general(left, right, dims, preferred_element_type=F32)


def inverse_rms(values):
    return lax.rsqrt(jnp.mean(values * values, axis=-1, keepdims=True) + NORM_EPS)


def rms_backward(scale_inv, normed, grad_normed):
    return scale_inv * (
        grad_normed - normed * jnp.mean(normed * grad_normed, axis=-1, keepdims=True)
    )


def adamw(weight, first, second, average, grad, rate):
    first_new = BETA * first + (1.0 - BETA) * grad
    second_new = BETA * second + (1.0 - BETA) * grad * grad
    fix = 1.0 - BETA**STEP
    weight_new = weight - rate * (
        first_new / fix / (jnp.sqrt(second_new / fix) + ADAM_EPS) + DECAY * weight
    )
    average_new = EMA_KEEP * average + (1.0 - EMA_KEEP) * weight_new
    return (first_new, second_new, weight_new, average_new)


def swap(value, axis, mask):
    size = lax.axis_size(axis)
    return lax.ppermute(value, axis, [(i, i ^ mask) for i in range(size)])


def digits_of(size):
    found = []
    stride = 1
    while stride < size:
        radix = 2 if stride == 1 or size // stride < 4 else 4
        found.append((stride, radix))
        stride *= radix
    return found


def gather_shards(shard, axis):
    size = lax.axis_size(axis)
    have = shard[None]
    for stride, radix in reversed(digits_of(size)):
        parts = [have] + [swap(have, axis, k * stride) for k in range(1, radix)]
        have = jnp.stack(parts, 1).reshape((-1,) + shard.shape)
    order = jnp.bitwise_xor(jnp.arange(size, dtype=jnp.int32), lax.axis_index(axis))
    return have.at[order].get(mode="promise_in_bounds")


def reduce_shards(blocks, axis, small_first):
    size = lax.axis_size(axis)
    order = jnp.bitwise_xor(jnp.arange(size, dtype=jnp.int32), lax.axis_index(axis))
    blocks = blocks.at[order].get(mode="promise_in_bounds")
    digits = digits_of(size)
    left = list(reversed(digits))
    blocks = blocks.reshape(tuple(radix for _, radix in left) + blocks.shape[1:])
    for at, (stride, radix) in enumerate(digits if small_first else reversed(digits)):
        place = left.index((stride, radix))
        left.pop(place)
        if at:
            blocks = blocks.astype(BF)
        pieces = [lax.index_in_dim(blocks, k, place, keepdims=False) for k in range(radix)]
        total = pieces[0].astype(F32)
        for k in range(1, radix):
            total = total + swap(pieces[k], axis, k * stride).astype(F32)
        blocks = total
    return blocks


def sum_everywhere(value, axis):
    size = lax.axis_size(axis)
    mask = 1
    while mask < size:
        value = value + swap(value, axis, mask)
        mask *= 2
    return value


def after(value, *first):
    return lax.optimization_barrier((value,) + first)[0]


def spread(matrix):
    high = matrix.astype(BF)
    low = (matrix - lax.optimization_barrier(high).astype(F32)).astype(BF)
    eye = jnp.eye(GROUP, dtype=BF)
    both = jnp.stack([high, low])
    count = matrix.shape[0] * GROUP
    wide = both[:, :, None, :, None] * eye[None, None, :, None, :]
    return wide.reshape(2 * count, count)


def two_heads(rows, first, second):
    return jnp.concatenate([rows * first, rows * second], 0)


def mix(matrix, values):
    out = dot(matrix, values)
    half = matrix.shape[0] // 2
    return out[:half] + out[half:]


def head_masks(scaling):
    lane = lax.broadcasted_iota(jnp.int32, (1, LANES), 1)
    low = lane < LANES // 2
    return low, jnp.where(low, scaling, 0.0).astype(BF), jnp.where(low, 0.0, scaling).astype(BF)


def fill_sequence(meta, sources, qkv, sems):
    me = meta[1]
    width = qkv.shape[1] // 3
    copies = []
    for part in range(3):
        for d in range(4):
            source = sources[4 * part + d]
            start = pl.multiple_of(jnp.bitwise_xor(me, d) * KEYS, KEYS)
            copies.append(
                pltpu.make_async_copy(
                    source,
                    qkv.at[pl.ds(start, KEYS), part * width : (part + 1) * width],
                    sems.at[4 * part + d],
                )
            )
    for copy in copies:
        copy.start()
    for copy in copies:
        copy.wait()


def forward_kernel(meta, *refs):
    sources, (pre, post, attended, probs, weights, qkv, held, sems) = refs[:12], refs[12:]
    heads = probs.shape[0]
    width = attended.shape[1]
    pairs = heads // 2
    tall = heads * GROUP
    step = pl.program_id(0)
    pl.when(step == 0)(partial(fill_sequence, meta, sources, qkv, sems))
    length = meta[0]
    row0 = pl.multiple_of(step * KEYS + meta[2] * ROWS, ROWS)
    chunks = (jnp.minimum(row0 + ROWS, length) + KEYS - 1) // KEYS
    low, first_s, second_s = head_masks(1.0 / math.sqrt(width // heads))

    def score(kc, carry):
        k0 = pl.multiple_of(kc * KEYS, KEYS)
        for p in range(pairs):
            at = p * LANES
            queries = two_heads(qkv[pl.ds(row0, ROWS), at : at + LANES], first_s, second_s)
            keys = qkv[pl.ds(k0, KEYS), width + at : width + at + LANES]
            scores = dot(queries, keys, NT).astype(BF)
            weights[2 * p : 2 * p + 2, :, pl.ds(k0, KEYS)] = scores.reshape(2, ROWS, KEYS)
        return carry

    lax.fori_loop(0, chunks, score, 0)

    def group(n, batch, carry):
        side = SIDE[n]
        rows = [
            pl.ds(pl.multiple_of((batch * side + u) * GROUP, GROUP), GROUP) for u in range(side)
        ]
        col_at = lax.broadcasted_iota(jnp.int32, (GROUP, KEYS), 1)
        row_at = lax.broadcasted_iota(jnp.int32, (GROUP, KEYS), 0)
        peak = [None] * side
        total = [None] * side
        for kc in range(n):
            cols = slice(kc * KEYS, (kc + 1) * KEYS)
            for u in range(side):
                mixed = mix(pre[...], weights[:, rows[u], cols].reshape(tall, KEYS))
                key_pos = col_at + kc * KEYS
                query_pos = row0 + (batch * side + u) * GROUP + row_at
                allowed = (key_pos <= query_pos) & (key_pos < length)
                mixed = jnp.where(allowed[None], mixed.reshape(heads, GROUP, KEYS), -1e30)
                mixed = mixed.reshape(tall, KEYS)
                held[u, :, cols] = mixed
                part = jnp.maximum(mixed[:, :LANES], mixed[:, LANES:])
                peak[u] = part if kc == 0 else jnp.maximum(peak[u], part)
        top = [jnp.max(peak[u], axis=1, keepdims=True) for u in range(side)]
        for kc in range(n):
            cols = slice(kc * KEYS, (kc + 1) * KEYS)
            for u in range(side):
                shifted = jnp.exp(held[u, :, cols] - top[u])
                held[u, :, cols] = shifted
                part = shifted[:, :LANES] + shifted[:, LANES:]
                total[u] = part if kc == 0 else total[u] + part
        inverse = [1.0 / jnp.sum(total[u], axis=1, keepdims=True) for u in range(side)]
        for kc in range(n):
            cols = slice(kc * KEYS, (kc + 1) * KEYS)
            for u in range(side):
                low_probs = (held[u, :, cols] * inverse[u]).astype(BF)
                probs[:, rows[u], cols] = low_probs.reshape(heads, GROUP, KEYS)
                mixed = mix(post[...], low_probs).astype(BF)
                weights[:, rows[u], cols] = mixed.reshape(heads, GROUP, KEYS)
        return carry

    def rest(n):
        lax.fori_loop(0, ROWS // GROUP // SIDE[n], partial(group, n), 0)
        for p in range(pairs):
            at = p * LANES
            pair = weights[2 * p : 2 * p + 2, :, : n * KEYS].reshape(2 * ROWS, n * KEYS)
            out = dot(pair, qkv[: n * KEYS, 2 * width + at : 2 * width + at + LANES])
            attended[:, at : at + LANES] = jnp.where(low, out[:ROWS], out[ROWS:]).astype(BF)

    for n in range(1, probs.shape[2] // KEYS + 1):
        pl.when(chunks == n)(partial(rest, n))


def backward_kernel(meta, *refs):
    sources, refs = refs[:12], refs[12:]
    grad_rows, pre, post, probs, weights, grad_q, grad_kv, grad_pre, grad_post = refs[:9]
    qkv, scores, grads, held, sum_pre, sum_post, sems = refs[9:]
    heads = probs.shape[0]
    width = grad_rows.shape[1]
    pairs = heads // 2
    tall = heads * GROUP
    step = pl.program_id(0)
    me = meta[1]

    @pl.when(step == 0)
    def _():
        grad_kv[...] = jnp.zeros_like(grad_kv)
        sum_pre[...] = jnp.zeros_like(sum_pre)
        sum_post[...] = jnp.zeros_like(sum_post)
        fill_sequence(meta, sources, qkv, sems)

    length = meta[0]
    row0 = pl.multiple_of(step * KEYS + meta[2] * ROWS, ROWS)
    chunks = (jnp.minimum(row0 + ROWS, length) + KEYS - 1) // KEYS
    chunks = jnp.where(row0 < length, chunks, 0)
    scaling = 1.0 / math.sqrt(width // heads)
    low, first_s, second_s = head_masks(scaling)
    low, first_one, second_one = head_masks(1.0)

    @pl.when(chunks == 0)
    def _():
        grad_q[...] = jnp.zeros_like(grad_q)

    def score(kc, carry):
        k0 = pl.multiple_of(kc * KEYS, KEYS)
        for p in range(pairs):
            at = p * LANES
            queries = two_heads(qkv[pl.ds(row0, ROWS), at : at + LANES], first_s, second_s)
            grad = two_heads(grad_rows[:, at : at + LANES], first_one, second_one)
            keys = qkv[pl.ds(k0, KEYS), width + at : width + at + LANES]
            values = qkv[pl.ds(k0, KEYS), 2 * width + at : 2 * width + at + LANES]
            both = slice(2 * p, 2 * p + 2)
            cols = pl.ds(k0, KEYS)
            scores[both, :, cols] = dot(queries, keys, NT).astype(BF).reshape(2, ROWS, KEYS)
            grads[both, :, cols] = dot(grad, values, NT).astype(BF).reshape(2, ROWS, KEYS)
        return carry

    lax.fori_loop(0, chunks, score, 0)

    def group(n, batch, carry):
        side = SIDE[n]
        rows = [
            pl.ds(pl.multiple_of((batch * side + u) * GROUP, GROUP), GROUP) for u in range(side)
        ]
        span = slice(0, n * KEYS)
        total = [None] * side
        for kc in range(n):
            cols = slice(kc * KEYS, (kc + 1) * KEYS)
            for u in range(side):
                grad_probs = mix(post[...], grads[:, rows[u], cols].reshape(tall, KEYS))
                held[u, :, cols] = grad_probs
                term = probs[:, rows[u], cols].reshape(tall, KEYS).astype(F32) * grad_probs
                part = term[:, :LANES] + term[:, LANES:]
                total[u] = part if kc == 0 else total[u] + part
        added = None
        for u in range(side):
            left = probs[:, rows[u], span].reshape(tall, n * KEYS)
            term = dot(left, grads[:, rows[u], span].reshape(tall, n * KEYS), NT)
            added = term if u == 0 else added + term
        sum_post[...] += added
        delta = [jnp.sum(total[u], axis=1, keepdims=True) for u in range(side)]
        mixed = [[] for _ in range(side)]
        for kc in range(n):
            cols = slice(kc * KEYS, (kc + 1) * KEYS)
            for u in range(side):
                prob = probs[:, rows[u], cols].reshape(tall, KEYS).astype(F32)
                grad_mixed = (prob * (held[u, :, cols] - delta[u])).astype(BF)
                mixed[u].append(grad_mixed)
                back = mix(pre[...], grad_mixed).astype(BF)
                grads[:, rows[u], cols] = back.reshape(heads, GROUP, KEYS)
        added = None
        for u in range(side):
            left = scores[:, rows[u], span].reshape(tall, n * KEYS)
            term = dot(left, jnp.concatenate(mixed[u], 1), NT)
            added = term if u == 0 else added + term
        sum_pre[...] += added
        return carry

    def rest(n):
        lax.fori_loop(0, ROWS // GROUP // SIDE[n], partial(group, n), 0)
        for p in range(pairs):
            at = p * LANES
            mine = slice(at, at + LANES)
            both = slice(2 * p, 2 * p + 2)
            queries = two_heads(qkv[pl.ds(row0, ROWS), mine], first_s, second_s).T
            grad = two_heads(grad_rows[:, mine], first_one, second_one).T
            back = grads[both, :, : n * KEYS].reshape(2 * ROWS, n * KEYS)
            out = dot(back, qkv[: n * KEYS, width + at : width + at + LANES])
            grad_q[:, mine] = (jnp.where(low, out[:ROWS], out[ROWS:]) * scaling).astype(BF)
            for kc in range(n):
                cols = slice(kc * KEYS, (kc + 1) * KEYS)
                d = jnp.bitwise_xor(me, kc)
                to = 2 * jnp.bitwise_and(d, 1) + d // 2
                grad_kv[to, mine, :] += dot(queries, grads[both, :, cols].reshape(2 * ROWS, KEYS))
                grad_kv[to, width + at : width + at + LANES, :] += dot(
                    grad, weights[both, :, cols].reshape(2 * ROWS, KEYS)
                )

    for n in range(1, probs.shape[2] // KEYS + 1):
        pl.when(chunks == n)(partial(rest, n))

    @pl.when(step == pl.num_programs(0) - 1)
    def _():
        row = lax.broadcasted_iota(jnp.int32, (tall, tall), 0)
        col = lax.broadcasted_iota(jnp.int32, (tall, tall), 1)
        same = row % GROUP == col % GROUP
        pick = (
            lax.broadcasted_iota(jnp.int32, (tall, LANES), 0) // GROUP
            == lax.broadcasted_iota(jnp.int32, (tall, LANES), 1)
        ).astype(F32)
        for source, out in ((sum_pre, grad_pre), (sum_post, grad_post)):
            kept = jnp.where(same, source[...], 0.0)
            wide = lax.dot_general(
                kept, pick, NN, precision=lax.Precision.HIGHEST, preferred_element_type=F32
            )
            for head in range(heads):
                out[head : head + 1, :] = jnp.sum(
                    wide[head * GROUP : (head + 1) * GROUP], axis=0, keepdims=True
                )


ANY = pl.BlockSpec(memory_space=pl.ANY)


def is_live(step, meta):
    return step * KEYS + meta[2] * ROWS < meta[0]


def attend(meta, sources, pre, post, heads):
    width = sources[0].shape[1]
    tall = heads * GROUP
    steps = 4
    full_len = steps * KEYS
    matrix = pl.BlockSpec((2 * tall, tall), lambda i, m: (0, 0), pipeline_mode=pl.Buffered(1))
    wide = pl.BlockSpec(
        (None, heads, ROWS, full_len), lambda i, m: (jnp.where(is_live(i, m), i, steps), 0, 0, 0)
    )
    kept = jax.ShapeDtypeStruct((steps + 1, heads, ROWS, full_len), BF)
    return pl.pallas_call(
        forward_kernel,
        grid_spec=pltpu.PrefetchScalarGridSpec(
            num_scalar_prefetch=1,
            grid=(steps,),
            in_specs=[ANY] * 12 + [matrix, matrix],
            out_specs=[
                pl.BlockSpec((None, ROWS, width), lambda i, m: (jnp.bitwise_xor(i, m[1]), 0, 0)),
                wide,
                wide,
            ],
            scratch_shapes=[
                pltpu.VMEM((full_len, 3 * width), BF),
                pltpu.VMEM((4, tall, full_len), F32),
                pltpu.SemaphoreType.DMA((12,)),
            ],
        ),
        out_shape=[jax.ShapeDtypeStruct((steps, ROWS, width), BF), kept, kept],
        compiler_params=pltpu.CompilerParams(vmem_limit_bytes=56 * 2**20),
        cost_estimate=pl.CostEstimate(
            flops=26 * 10**9, bytes_accessed=30 * 10**6, transcendentals=0
        ),
        name="attend",
    )(meta, *sources, pre, post)


def attend_back(meta, sources, grad_rows, pre, post, probs, weights):
    width = sources[0].shape[1]
    steps = 4
    heads = probs.shape[1]
    tall = heads * GROUP
    full_len = steps * KEYS

    def newest(step, meta):
        last = 0
        for other in range(1, steps):
            last = jnp.where(is_live(other, meta), other, last)
        return jnp.minimum(step, last)

    matrix = pl.BlockSpec((2 * tall, tall), lambda i, m: (0, 0), pipeline_mode=pl.Buffered(1))
    wide = pl.BlockSpec((None, heads, ROWS, full_len), lambda i, m: (newest(i, m), 0, 0, 0))
    rows = pl.BlockSpec((None, ROWS, width), lambda i, m: (jnp.bitwise_xor(i, m[1]), 0, 0))
    small = pl.BlockSpec((heads, LANES), lambda i, m: (0, 0))
    return pl.pallas_call(
        backward_kernel,
        grid_spec=pltpu.PrefetchScalarGridSpec(
            num_scalar_prefetch=1,
            grid=(steps,),
            in_specs=[ANY] * 12 + [rows, matrix, matrix, wide, wide],
            out_specs=[
                rows,
                pl.BlockSpec(
                    (4, 2 * width, KEYS), lambda i, m: (0, 0, 0), pipeline_mode=pl.Buffered(1)
                ),
                small,
                small,
            ],
            scratch_shapes=[
                pltpu.VMEM((full_len, 3 * width), BF),
                pltpu.VMEM((heads, ROWS, full_len), BF),
                pltpu.VMEM((heads, ROWS, full_len), BF),
                pltpu.VMEM((4, tall, full_len), F32),
                pltpu.VMEM((tall, tall), F32),
                pltpu.VMEM((tall, tall), F32),
                pltpu.SemaphoreType.DMA((12,)),
            ],
        ),
        out_shape=[
            jax.ShapeDtypeStruct((steps, ROWS, width), BF),
            jax.ShapeDtypeStruct((4, 2 * width, KEYS), F32),
            jax.ShapeDtypeStruct((heads, LANES), F32),
            jax.ShapeDtypeStruct((heads, LANES), F32),
        ],
        compiler_params=pltpu.CompilerParams(vmem_limit_bytes=60 * 2**20),
        cost_estimate=pl.CostEstimate(
            flops=40 * 10**9, bytes_accessed=40 * 10**6, transcendentals=0
        ),
        name="attend_back",
    )(meta, *sources, grad_rows, pre, post, probs, weights)


def on_device(
    tokens,
    cotangent,
    lengths,
    qkv_weight,
    qkv_first,
    qkv_second,
    qkv_average,
    proj_weight,
    proj_first,
    proj_second,
    proj_average,
    inner_weight,
    inner_first,
    inner_second,
    inner_average,
    outer_weight,
    outer_first,
    outer_second,
    outer_average,
    gains,
    gain_first,
    gain_second,
    gain_average,
    mixes,
    mix_first,
    mix_second,
    mix_average,
):
    group_seqs, shard_len, width = tokens.shape
    owners = lax.axis_size("dp")
    heads = mixes.shape[1]
    own_rows = qkv_weight.shape[0]
    hidden = inner_weight.shape[1]
    half = width // 2
    slice_ff = hidden // owners // 2
    me = lax.axis_index("seq")
    pair = me // 2
    core = jnp.bitwise_and(me, 1)

    def by_core(mine, other, axis):
        return jnp.where(
            core == 0,
            jnp.concatenate([mine, other], axis),
            jnp.concatenate([other, mine], axis),
        )

    ahead = (lengths[None, :] > lengths[:, None]) | (
        (lengths[None, :] == lengths[:, None])
        & (jnp.arange(group_seqs)[None, :] < jnp.arange(group_seqs)[:, None])
    )
    rank = jnp.sum(ahead.astype(jnp.int32), axis=1)
    order = jnp.sum(
        jnp.where(
            rank[None, :] == jnp.arange(group_seqs)[:, None], jnp.arange(group_seqs)[None, :], 0
        ),
        axis=1,
    ).astype(jnp.int32)

    def sequence_of(slot, which):
        return order[which if slot == 0 else group_seqs - 1 - which]

    def arrange(value):
        return jnp.stack(
            [
                jnp.stack(
                    [
                        lax.dynamic_index_in_dim(
                            value, sequence_of(slot, jnp.bitwise_xor(pair, d)), 0, False
                        )
                        for d in range(2)
                    ]
                )
                for slot in range(2)
            ]
        )

    def restore(value):
        flat = value.reshape((4,) + value.shape[2:])
        which = jnp.where(rank < 2, rank, 3 - rank)
        place = 2 * (rank // 2) + jnp.bitwise_xor(which, pair)
        return flat.at[place].get(mode="promise_in_bounds")

    lengths_here = arrange(lengths)
    metas = [jnp.stack([lengths_here[slot, 0], me, core]).astype(jnp.int32) for slot in range(2)]

    gain_low = gather_shards(gains.astype(BF), "dp")
    gain_vals = jnp.moveaxis(gain_low, 0, 1).reshape(2, width).astype(F32)
    qkv_low = qkv_weight.astype(BF)
    gathered = []
    gate = None
    for part in range(3):
        mine = lax.dynamic_slice_in_dim(qkv_low, part * width + core * half, half, 1)
        if gate is not None:
            mine = after(mine, gate)
        whole = gather_shards(mine, "dp").reshape(owners * own_rows, half)
        gate = whole
        gathered.append(by_core(whole, swap(whole, "seq", 1), 1))

    proj_low = after(proj_weight.astype(BF), gate)
    inner_mine = inner_weight.astype(BF).reshape(own_rows, owners, 2, slice_ff)
    inner_mine = lax.dynamic_index_in_dim(inner_mine, core, 2, False)
    inner_mine = inner_mine.reshape(own_rows, owners * slice_ff)
    outer_mine = outer_weight.astype(BF).reshape(2, slice_ff, width)
    outer_mine = lax.dynamic_index_in_dim(outer_mine, core, 0, False)
    proj_all = lax.all_gather(proj_low, "dp", axis=0, tiled=True)
    inner_halves = [lax.all_gather(after(inner_mine, gate), "dp", axis=0, tiled=True)]
    outer_halves = [lax.all_gather(after(outer_mine, gate), "dp", axis=0, tiled=True)]
    inner_halves.append(swap(inner_halves[0], "seq", 1))
    outer_halves.append(swap(outer_halves[0], "seq", 1))

    input_rows = arrange(tokens).astype(F32)
    scale_one = inverse_rms(input_rows)
    normed_one = input_rows * scale_one
    first_in = (normed_one * gain_vals[0]).astype(BF)
    sources = [[None] * 12, [None] * 12]
    gate = None
    for slot in range(2):
        for part in range(3):
            far = dot(first_in[slot, 1], gathered[part]).astype(BF)
            if gate is not None:
                far = after(far, gate)
            near = dot(first_in[slot, 0], gathered[part]).astype(BF)
            far = swap(far, "seq", 2)
            sources[slot][4 * part : 4 * part + 4] = [
                near,
                swap(near, "seq", 1),
                far,
                swap(far, "seq", 1),
            ]
        gate = far

    pre_mix, post_mix = spread(mixes[0].T), spread(mixes[1].T)
    pre_back, post_back = spread(mixes[0]), spread(mixes[1])

    def to_homes(rows):
        got = [rows[0]] + [swap(rows[d], "seq", d) for d in range(1, 4)]
        return jnp.stack([by_core(got[2 * d], got[2 * d + 1], 0) for d in range(2)])

    def from_homes(rows):
        halves = rows.reshape(2, 2, ROWS, width)
        found = []
        for d in range(4):
            block = lax.dynamic_index_in_dim(
                halves[d // 2], jnp.bitwise_xor(core, d % 2), 0, False
            )
            found.append(swap(block, "seq", d) if d else block)
        return jnp.stack(found)

    attended, probs, weights = [], [], []
    meta = metas[0]
    for slot in range(2):
        out, prob, weight = attend(meta, sources[slot], pre_mix, post_mix, heads)
        if slot == 0:
            meta, out = lax.optimization_barrier((metas[1], out))
        attended.append(to_homes(out))
        probs.append(prob)
        weights.append(weight)
    attention_output = jnp.stack(attended)

    resid = input_rows + jnp.einsum(
        "sdrk,kc->sdrc", attention_output, proj_all, preferred_element_type=F32
    )
    scale_two = inverse_rms(resid)
    normed_two = resid * scale_two
    second_in = (normed_two * gain_vals[1]).astype(BF)
    positions = me * shard_len + jnp.arange(shard_len, dtype=jnp.int32)
    live = positions[None, None, :] < lengths_here[:, :, None]
    cot = arrange(cotangent)
    grad_out = jnp.where(live[..., None], cot, jnp.zeros_like(cot))
    output = resid
    grad_second = 0.0
    grad_inner, grad_outer = [], []
    for inner, outer in zip(inner_halves, outer_halves):
        hidden_state = jnp.einsum("sdrk,kf->sdrf", second_in, inner, preferred_element_type=F32)
        active, gelu_back = jax.vjp(partial(jax.nn.gelu, approximate=True), hidden_state)
        active = active.astype(BF)
        output = output + jnp.einsum(
            "sdrf,fk->sdrk", active, outer, preferred_element_type=F32
        )
        grad_outer.append(
            jnp.einsum("sdrf,sdrk->fk", active, grad_out, preferred_element_type=F32)
        )
        grad_active = jnp.einsum("sdrk,fk->sdrf", grad_out, outer, preferred_element_type=F32)
        grad_hidden = gelu_back(grad_active)[0].astype(BF)
        grad_inner.append(
            jnp.einsum("sdrk,sdrf->kf", second_in, grad_hidden, preferred_element_type=F32)
        )
        grad_second = grad_second + jnp.einsum(
            "sdrf,kf->sdrk", grad_hidden, inner, preferred_element_type=F32
        )
    output = output.astype(BF)
    gain_two = jnp.sum(grad_second * normed_two, axis=(0, 1, 2))
    grad_resid = grad_out.astype(F32) + rms_backward(
        scale_two, normed_two, grad_second * gain_vals[1]
    )
    resid_low = grad_resid.astype(BF)
    grad_attended = jnp.einsum(
        "sdrc,kc->sdrk", resid_low, proj_all, preferred_element_type=F32
    ).astype(BF)
    grad_proj = jnp.einsum(
        "sdrk,sdrc->kc", attention_output, resid_low, preferred_element_type=F32
    )

    def reduce_halves(mine, other, small_first):
        total = mine + swap(other.astype(BF), "seq", 1).astype(F32)
        total = reduce_shards(total.astype(BF), "dp", small_first)
        total = lax.optimization_barrier(total.astype(BF))
        total = total.astype(F32) + swap(total, "seq", 2).astype(F32)
        return total, swap(total, "seq", 1)

    grad_proj = grad_proj.reshape(owners, own_rows, 2, half)
    proj_mine, proj_other = reduce_halves(
        lax.dynamic_index_in_dim(grad_proj, core, 2, False),
        lax.dynamic_index_in_dim(grad_proj, 1 - core, 2, False),
        True,
    )
    red_proj = by_core(proj_mine, proj_other, 1)
    inner_sums = reduce_halves(
        *[g.reshape(owners, own_rows, owners * slice_ff) for g in grad_inner], True
    )
    red_inner = by_core(
        *[g.reshape(own_rows, owners, 1, slice_ff) for g in inner_sums], 2
    ).reshape(own_rows, hidden)
    outer_sums = reduce_halves(
        *[g.reshape(owners, slice_ff, width) for g in grad_outer], False
    )
    red_outer = by_core(*outer_sums, 0)

    grad_rows = [from_homes(grad_attended[slot]) for slot in range(2)]
    meta = metas[0]
    grad_mixes = 0.0
    grad_q, grad_kv = [], []
    for slot in range(2):
        back_q, back_kv, back_pre, back_post = attend_back(
            meta, sources[slot], grad_rows[slot], pre_back, post_back, probs[slot], weights[slot]
        )
        if slot == 0:
            meta, back_kv = lax.optimization_barrier((metas[1], back_kv))
        grad_mixes = grad_mixes + jnp.stack([back_pre[:, :heads], back_post[:, :heads]])
        summed = (back_kv[:2] + swap(back_kv[2:], "seq", 1)).astype(BF)
        grad_kv.append(jnp.stack([summed[0], swap(summed[1], "seq", 2)]))
        grad_q.append(to_homes(back_q))

    grad_first = []
    grad_qkv = 0.0
    weight_kv = jnp.concatenate(gathered[1:], axis=1)
    for slot in range(2):
        grad_first.append(
            jnp.einsum("drk,ck->drc", grad_q[slot], gathered[0], preferred_element_type=F32)
            + jnp.einsum("dkr,ck->drc", grad_kv[slot], weight_kv, preferred_element_type=F32)
        )
        grad_qkv = grad_qkv + jnp.concatenate(
            [
                jnp.einsum("drc,drk->ck", first_in[slot], grad_q[slot], preferred_element_type=F32),
                jnp.einsum(
                    "drc,dkr->ck", first_in[slot], grad_kv[slot], preferred_element_type=F32
                ),
            ],
            axis=1,
        )
    grad_first = jnp.stack(grad_first)
    gain_one = jnp.sum(grad_first * normed_one, axis=(0, 1, 2))
    grad_qkv = grad_qkv.reshape(owners, own_rows, 3, 2, half)
    mine = lax.dynamic_index_in_dim(grad_qkv, core, 3, False)
    other = lax.dynamic_index_in_dim(grad_qkv, 1 - core, 3, False)
    q_sums = reduce_halves(mine[:, :, :1], other[:, :, :1], False)
    kv_sums = reduce_halves(mine[:, :, 1:], other[:, :, 1:], True)
    red_qkv = jnp.concatenate(
        [
            by_core(*[g[..., None, :] for g in sums], 2)
            for sums in (q_sums, kv_sums)
        ],
        axis=1,
    ).reshape(own_rows, 3 * width)

    small = jnp.concatenate([gain_one, gain_two, grad_mixes.reshape(-1)])
    pad = -small.shape[0] % (8 * LANES)
    small = jnp.pad(small, (0, pad)).reshape(-1, LANES)
    small = sum_everywhere(sum_everywhere(small, "seq"), "dp").reshape(-1)
    own = lax.axis_index("dp")
    red_gains = lax.dynamic_slice_in_dim(
        small[: 2 * width].reshape(2, width), own * own_rows, own_rows, 1
    )
    gain_all = small[: 2 * width]
    red_mixes = small[2 * width : 2 * width + grad_mixes.size].reshape(mixes.shape)

    grad_rows_tokens = grad_resid + rms_backward(
        scale_one, normed_one, grad_first * gain_vals[0]
    )

    local_squares = (
        jnp.sum(red_qkv * red_qkv)
        + jnp.sum(red_proj * red_proj)
        + jnp.sum(red_inner * red_inner)
        + jnp.sum(red_outer * red_outer)
    )
    total_squares = sum_everywhere(jnp.broadcast_to(local_squares, (8, LANES)), "dp")[0, 0]
    grad_norm = jnp.sqrt(
        total_squares + jnp.sum(gain_all * gain_all) + jnp.sum(red_mixes * red_mixes)
    )
    factor = CLIP / jnp.maximum(grad_norm, CLIP)
    clipped_gains = red_gains * factor
    qkv_new = adamw(qkv_weight, qkv_first, qkv_second, qkv_average, red_qkv * factor, 0.03)
    proj_new = adamw(proj_weight, proj_first, proj_second, proj_average, red_proj * factor, 0.1)
    inner_new = adamw(
        inner_weight, inner_first, inner_second, inner_average, red_inner * factor, 0.03
    )
    outer_new = adamw(
        outer_weight, outer_first, outer_second, outer_average, red_outer * factor, 0.02
    )
    gain_new = adamw(gains, gain_first, gain_second, gain_average, clipped_gains, 0.3)
    mix_new = adamw(mixes, mix_first, mix_second, mix_average, red_mixes * factor, 0.3)
    return (
        restore(output),
        restore(grad_rows_tokens),
        grad_norm,
        *qkv_new,
        *proj_new,
        *inner_new,
        *outer_new,
        *gain_new,
        *mix_new,
        clipped_gains,
    )


def solution(mesh):
    rows = P("dp", "seq", None)
    matrix = P("dp", None)
    vector = P(None, "dp")
    in_specs = (rows, rows, P("dp")) + (matrix,) * 16 + (vector,) * 4 + (P(),) * 4
    out_specs = (rows, rows, P()) + (matrix,) * 16 + (vector,) * 4 + (P(),) * 4 + (vector,)
    return jax.shard_map(
        on_device, mesh=mesh, in_specs=in_specs, out_specs=out_specs, check_vma=False
    )
```

time: 2010 us -> 754 us (0.38)
  matrix products: 588 us -> 106 us
  other arithmetic: 522 us -> 97.1 us
  local copies, waits for them, and re-layouts: 346 us -> 127 us
  waiting for transfers between devices: 353 us -> 154 us
  blocking collectives: 131 us -> 0 us
  Pallas kernels: 0 us -> 125 us
  starting transfers between devices: 14.5 us -> 114 us
  loops' own time: 22.3 us -> 0 us
    dot_general x30 -> x35, matrix products: 588 us -> 106 us  [the longest x12 16.4 us: dot(): return lax.dot_general(left, right, dims, preferred_element_type=F32)]
    convert_element_type x13 -> x26, other arithmetic: 192 us -> 29.5 us  [the longest x5 13.6 us: reduce_halves(): total = reduce_shards(total.astype(BF), 'dp', small_first)]
    ppermute x0 -> x104, waiting for transfers between devices: none -> 154 us  [swap(): return lax.ppermute(value, axis, [(i, i ^ mask) for i in range(size)])]
    pallas_call x0 -> x4, Pallas kernels: none -> 125 us  [the longest x2 66.8 us: attend_back(): pl.pallas_call(backward_kernel, grid_spec=pltpu.PrefetchScalarGridSpec(nu...]
    mul x56 -> x14, local copies, waits for them, and re-layouts: 137 us -> 20.5 us  [the longest x8 14.1 us: spread(): wide = both[:, :, None, :, None] * eye[None, None, :, None, :]]
    reduce_scatter x4 -> x0, waiting for transfers between devices: 116 us -> none  [the longest x1 116 us: on_device(): lax.psum_scatter(query_key_value_gradient, 'dp', scatter_dimension=0, til...]
    ppermute x0 -> x104, starting transfers between devices: none -> 114 us  [swap(): return lax.ppermute(value, axis, [(i, i ^ mask) for i in range(size)])]
    mul x12 -> x4, other arithmetic: 104 us -> 3.73 us  [the longest x1 2.59 us: spread(): wide = both[:, :, None, :, None] * eye[None, None, :, None, :]]
  transfers between devices with their start and end apart: 13 -> 107, of which waited for: 7 -> 32; matrix products, arithmetic and copies ran while one was open for 69% -> 36% of each run, Pallas kernels for 0% -> 17%
where the time goes in v1:
time: 754 us; the launch traced here: 752 us
  waiting for transfers between devices  154 us (20%)
  local copies, waits for them, and re-layouts  127 us (17%)
  Pallas kernels  125 us (17%)
  starting transfers between devices  114 us (15%)
  matrix products  106 us (14%)
  other arithmetic  97.1 us (13%)
  between operations  29.8 us (4%)
    ppermute x104, waiting for transfers between devices, swap(): return lax.ppermute(value, axis, [(i, i ^ mask) for i in range(size)])  154 us
    ppermute x104, starting transfers between devices, swap(): return lax.ppermute(value, axis, [(i, i ^ mask) for i in range(size)])  114 us
    pallas_call x2, Pallas kernels, attend_back(): pl.pallas_call(backward_kernel, grid_spec=pltpu.PrefetchScalarGridSpec(nu...  66.8 us
    pallas_call x2, Pallas kernels, attend(): pl.pallas_call(forward_kernel, grid_spec=pltpu.PrefetchScalarGridSpec(num...  58 us
    dot_general x12, matrix products, dot(): return lax.dot_general(left, right, dims, preferred_element_type=F32)  16.4 us
  transfers between devices with their start and end apart: 107, of which 32 were waited for; matrix products, arithmetic and copies ran while one was open for 36% of the time, Pallas kernels for 17%

profile of v1, /device:TPU:0, one launch (start us, length us, event | category | flops | bytes accessed | tf_op | source)
XLA Modules:
  0.0 752.4 jit_solution(945849133149140590)
XLA Ops:
  78.1 5.8 collective-permute-done.23
  133.9 7.5 %collective-permute-done.26.refs_10_ = bf16[256,768]{1,0:T(8,128)(2,1)S(1)} collective-permute-done((bf16[256,768]{1,0:T(8,128)(2,1)S(1)}, bf16[256,768]{1,0:T(8,128)(2,1)S(1)}, u32[]{:S(2)}, u32[]{:S(2)}) %collective-permute-start.26) | collective-permute-done | bytes 393248 | tf_op jit(solution)/shard_map/ppermute | solution.py:59
  148.1 29.7 %attend.2 = (bf16[4,128,768]{2,1,0:T(8,128)(2,1)}, bf16[5,12,128,1024]{3,2,1,0:T(8,128)(2,1)}, bf16[5,12,128,1024]{3,2,1,0:T(8,128)(2,1)}) custom-call(s32[3]{0:T(128)} %add_add_fusion.1.meta, bf16[256,768]{1,0:T(8,128)(2,1)} %copy-done.120, bf16[256,768]{1,0:T(8,128)(2,1)} %collective-permute-done.9.refs_1_, bf16[256,768]{1,0:T(8,128)(2,1)} %copy-done.119, ...), custom_call_target="tpu_custom_call" | custom-call | flops 25999998976 | bytes 30000000 | tf_op jit(solution)/shard_map/attend/pallas_call | solution.py:383
  192.0 28.3 %attend.3 = (bf16[4,128,768]{2,1,0:T(8,128)(2,1)}, bf16[5,12,128,1024]{3,2,1,0:T(8,128)(2,1)}, bf16[5,12,128,1024]{3,2,1,0:T(8,128)(2,1)}) custom-call(s32[3]{0:T(128)} %add_add_fusion.meta, bf16[256,768]{1,0:T(8,128)(2,1)} %convolution_convert_fusion.6.refs_0_, bf16[256,768]{1,0:T(8,128)(2,1)} %copy-done.125, ...), custom_call_target="tpu_custom_call" | custom-call | flops 25999998976 | bytes 30000000 | tf_op jit(solution)/shard_map/attend/pallas_call | solution.py:383
  240.4 5.7 multiply_convert_fusion.1
  246.2 6.2 fusion.6
  273.9 6.4 fusion.13
  284.3 5.4 multiply_reduce_fusion
  312.0 7.4 add_convert_fusion.4
  329.3 38.0 %attend_back.2 = (bf16[4,128,768]{2,1,0:T(8,128)(2,1)}, f32[4,1536,256]{2,1,0:T(8,128)}, f32[12,128]{1,0:T(8,128)}, f32[12,128]{1,0:T(8,128)}) custom-call(s32[3]{0:T(128)} %add_add_fusion.1.meta, bf16[256,768]{1,0:T(8,128)(2,1)} %copy-done.120, bf16[256,768]{1,0:T(8,128)(2,1)} %collective-permute-done.9.refs_1_, bf16[256,768]{1,0:T(8,128)(2,1)} %copy-done.119, ...), custom_call_target="tpu_custom_call" | custom-call | flops 40000000000 | bytes 40000000 | tf_op jit(solution)/shard_map/attend_back/pallas_call | solution.py:426
  369.7 28.7 %attend_back.3 = (bf16[4,128,768]{2,1,0:T(8,128)(2,1)}, f32[4,1536,256]{2,1,0:T(8,128)}, f32[12,128]{1,0:T(8,128)}, f32[12,128]{1,0:T(8,128)}) custom-call(s32[3]{0:T(128)} %add_add_fusion.meta, bf16[256,768]{1,0:T(8,128)(2,1)} %convolution_convert_fusion.6.refs_0_, bf16[256,768]{1,0:T(8,128)(2,1)} %copy-done.125, ...), custom_call_target="tpu_custom_call" | custom-call | flops 40000000000 | bytes 40000000 | tf_op jit(solution)/shard_map/attend_back/pallas_call | solution.py:426
  468.7 14.8 %collective-permute-done.90 = bf16[2,192,768]{2,1,0:T(8,128)(2,1)} collective-permute-done((bf16[2,192,768]{2,1,0:T(8,128)(2,1)}, bf16[2,192,768]{2,1,0:T(8,128)(2,1)}, u32[]{:S(2)}, u32[]{:S(2)}) %collective-permute-start.90) | collective-permute-done | bytes 589856 | tf_op jit(solution)/shard_map/ppermute | solution.py:59
  483.5 15.6 %collective-permute-done.91 = bf16[2,192,768]{2,1,0:T(8,128)(2,1)} collective-permute-done((bf16[2,192,768]{2,1,0:T(8,128)(2,1)S(1)}, bf16[2,192,768]{2,1,0:T(8,128)(2,1)}, u32[]{:S(2)}, u32[]{:S(2)}) %collective-permute-start.91) | collective-permute-done | bytes 589856 | tf_op jit(solution)/shard_map/ppermute | solution.py:59
  503.3 7.8 %collective-permute-done.93 = bf16[192,768]{1,0:T(8,128)(2,1)S(1)} collective-permute-done((bf16[192,768]{1,0:T(8,128)(2,1)S(1)}, bf16[192,768]{1,0:T(8,128)(2,1)S(1)}, u32[]{:S(2)}, u32[]{:S(2)}) %collective-permute-start.93) | collective-permute-done | bytes 294944 | tf_op jit(solution)/shard_map/ppermute | solution.py:59
  517.5 17.1 %collective-permute-done.83 = bf16[4,96,1536]{2,1,0:T(8,128)(2,1)S(1)} collective-permute-done((bf16[4,96,1536]{2,1,0:T(8,128)(2,1)S(1)}, bf16[4,96,1536]{2,1,0:T(8,128)(2,1)S(1)}, u32[]{:S(2)}, u32[]{:S(2)}) %collective-permute-start.83) | collective-permute-done | bytes 1179680 | tf_op jit(solution)/shard_map/ppermute | solution.py:59
  535.0 13.3 %collective-permute-start.84 = (bf16[96,1536]{1,0:T(8,128)(2,1)S(1)}, bf16[96,1536]{1,0:T(8,128)(2,1)S(1)}, u32[]{:S(2)}, u32[]{:S(2)}) collective-permute-start(bf16[96,1536]{1,0:T(8,128)(2,1)S(1)} %get-tuple-element.216), channel_id=1, source_target_pairs={{0,8},{4,12},{8,0},{12,4},{16,24},{20,28},{24,16},{28,20},{1,9},{5... | collective-permute-start | bytes 884744 | tf_op jit(solution)/shard_map/ppermute | solution.py:59
  552.9 6.0 collective-permute-done.84
  558.9 12.8 %collective-permute-done.85 = bf16[96,1536]{1,0:T(8,128)(2,1)S(1)} collective-permute-done((bf16[96,1536]{1,0:T(8,128)(2,1)S(1)}, bf16[96,1536]{1,0:T(8,128)(2,1)S(1)}, u32[]{:S(2)}, u32[]{:S(2)}) %collective-permute-start.85) | collective-permute-done | bytes 294944 | tf_op jit(solution)/shard_map/ppermute | solution.py:59
  575.1 6.8 collective-permute-done.87
  609.3 9.7 %add.497 = f32[8,96,3,2,384]{4,3,2,1,0:T(2,128)} reshape(f32[768,2304]{1,0:T(8,128)} %maximum_add_fusion) | data formatting | bytes 14155776 | tf_op jit(solution)/shard_map/add | solution.py:716
  620.9 6.2 constant_dynamic-slice_fusion.3
  629.0 6.6 constant_dynamic-slice_fusion.4
  636.1 7.9 %collective-permute-start.102 = (f32[16,128]{1,0:T(8,128)S(1)}, f32[16,128]{1,0:T(8,128)S(1)}, u32[]{:S(2)}, u32[]{:S(2)}) collective-permute-start(f32[16,128]{1,0:T(8,128)S(1)} %add.539), channel_id=1, source_target_pairs={{0,8},{4,12},{8,0},{12,4},{16,24},{20,28},{24,16},{28,20},{1,9},{5... | collective-permute-start | bytes 24584 | tf_op jit(solution)/shard_map/ppermute | solution.py:59
  697.5 6.8 fusion.22
  (714 shorter events, 422.1 us)
Async XLA Ops:
  7.2 226.4 %all-gather.4.cloned.1.call-start = ((), (), s32[]{:S(2)}) async-start(), calls=%async_computation | async-start | bytes 1327104 | tf_op jit(solution)/shard_map/all_gather | solution.py:569
  15.5 85.4 %collective-permute-start = (bf16[1,2,96]{2,1,0:T(2,128)(2,1)}, bf16[1,2,96]{2,1,0:T(2,128)(2,1)}, u32[]{:S(2)}, u32[]{:S(2)}) collective-permute-start(bf16[1,2,96]{2,1,0:T(2,128)(2,1)} %get-tuple-element.283), channel_id=1, source_target_pairs={{0,8},{4,12},{8,0},{12,4},{16,24},{20,28},{24,16},{28,20},{1,9},{5... | collective-permute-start | bytes 1160 | tf_op jit(solution)/shard_map/ppermute | solution.py:59
  16.4 84.5 %collective-permute-start.1 = (bf16[1,2,96]{2,1,0:T(2,128)(2,1)}, bf16[1,2,96]{2,1,0:T(2,128)(2,1)}, u32[]{:S(2)}, u32[]{:S(2)}) collective-permute-start(bf16[1,2,96]{2,1,0:T(2,128)(2,1)} %get-tuple-element.283), channel_id=1, source_target_pairs={{0,16},{4,20},{8,24},{12,28},{16,0},{20,4},{24,8},{28,12},{1,17},{... | collective-permute-start | bytes 1160 | tf_op jit(solution)/shard_map/ppermute | solution.py:59
  87.3 151.8 %all-gather.6.cloned.1.call-start = ((), (), s32[]{:S(2)}) async-start(), calls=%async_computation.1 | async-start | bytes 2654208 | tf_op jit(solution)/shard_map/all_gather | solution.py:570
  119.8 120.5 %all-gather.8.cloned.1.call-start = ((), (), s32[]{:S(2)}) async-start(), calls=%async_computation.2 | async-start | bytes 2654208 | tf_op jit(solution)/shard_map/all_gather | solution.py:571
  144.0 37.1 %collective-permute-start.31 = (bf16[256,768]{1,0:T(8,128)(2,1)}, bf16[256,768]{1,0:T(8,128)(2,1)S(1)}, u32[]{:S(2)}, u32[]{:S(2)}) collective-permute-start(bf16[256,768]{1,0:T(8,128)(2,1)} %convolution_convert_fusion.6.refs_0_), channel_id=1, source_target_pairs={{0,1},{1,0},{2,3},{3,2},{4,5},{5,4},{6,7},{7,6},{8,9},{9,8},{10,11... | collective-permute-start | bytes 1179656 | tf_op jit(solution)/shard_map/ppermute | solution.py:59
  144.5 37.1 %collective-permute-start.38 = (bf16[256,768]{1,0:T(8,128)(2,1)}, bf16[256,768]{1,0:T(8,128)(2,1)}, u32[]{:S(2)}, u32[]{:S(2)}) collective-permute-start(bf16[256,768]{1,0:T(8,128)(2,1)} %convolution_convert_fusion.1), channel_id=1, source_target_pairs={{0,2},{1,3},{2,0},{3,1},{4,6},{5,7},{6,4},{7,5},{8,10},{9,11},{10,... | collective-permute-start | bytes 1179656 | tf_op jit(solution)/shard_map/ppermute | solution.py:59
  145.1 36.6 %collective-permute-start.35 = (bf16[256,768]{1,0:T(8,128)(2,1)}, bf16[256,768]{1,0:T(8,128)(2,1)}, u32[]{:S(2)}, u32[]{:S(2)}) collective-permute-start(bf16[256,768]{1,0:T(8,128)(2,1)} %convolution_convert_fusion.3), channel_id=1, source_target_pairs={{0,2},{1,3},{2,0},{3,1},{4,6},{5,7},{6,4},{7,5},{8,10},{9,11},{10,... | collective-permute-start | bytes 1179656 | tf_op jit(solution)/shard_map/ppermute | solution.py:59
  146.6 35.5 %collective-permute-start.32 = (bf16[256,768]{1,0:T(8,128)(2,1)S(1)}, bf16[256,768]{1,0:T(8,128)(2,1)}, u32[]{:S(2)}, u32[]{:S(2)}) collective-permute-start(bf16[256,768]{1,0:T(8,128)(2,1)S(1)} %copy-done.133), channel_id=1, source_target_pairs={{0,2},{1,3},{2,0},{3,1},{4,6},{5,7},{6,4},{7,5},{8,10},{9,11},{10,... | collective-permute-start | bytes 1179656 | tf_op jit(solution)/shard_map/ppermute | solution.py:59
  297.5 69.8 %collective-permute-start.53 = (bf16[128,768]{1,0:T(8,128)(2,1)}, bf16[128,768]{1,0:T(8,128)(2,1)}, u32[]{:S(2)}, u32[]{:S(2)}) collective-permute-start(bf16[128,768]{1,0:T(8,128)(2,1)} %get-tuple-element.246), channel_id=1, source_target_pairs={{0,1},{1,0},{2,3},{3,2},{4,5},{5,4},{6,7},{7,6},{8,9},{9,8},{10,11... | collective-permute-start | bytes 589832 | tf_op jit(solution)/shard_map/ppermute | solution.py:59
  298.9 68.8 %collective-permute-start.54 = (bf16[128,768]{1,0:T(8,128)(2,1)}, bf16[128,768]{1,0:T(8,128)(2,1)}, u32[]{:S(2)}, u32[]{:S(2)}) collective-permute-start(bf16[128,768]{1,0:T(8,128)(2,1)} %get-tuple-element.247), channel_id=1, source_target_pairs={{0,2},{1,3},{2,0},{3,1},{4,6},{5,7},{6,4},{7,5},{8,10},{9,11},{10,... | collective-permute-start | bytes 589832 | tf_op jit(solution)/shard_map/ppermute | solution.py:59
  326.1 41.5 %collective-permute-start.55 = (bf16[128,768]{1,0:T(8,128)(2,1)S(1)}, bf16[128,768]{1,0:T(8,128)(2,1)S(1)}, u32[]{:S(2)}, u32[]{:S(2)}) collective-permute-start(bf16[128,768]{1,0:T(8,128)(2,1)S(1)} %copy-done.82), channel_id=1, source_target_pairs={{0,3},{1,2},{2,1},{3,0},{4,7},{5,6},{6,5},{7,4},{8,11},{9,10},{10,... | collective-permute-start | bytes 589832 | tf_op jit(solution)/shard_map/ppermute | solution.py:59
  326.7 122.0 %collective-permute-start.89 = (bf16[8,192,768]{2,1,0:T(8,128)(2,1)}, bf16[8,192,768]{2,1,0:T(8,128)(2,1)}, u32[]{:S(2)}, u32[]{:S(2)}) collective-permute-start(bf16[8,192,768]{2,1,0:T(8,128)(2,1)} %bitcast.562), channel_id=1, source_target_pairs={{0,1},{1,0},{2,3},{3,2},{4,5},{5,4},{6,7},{7,6},{8,9},{9,8},{10,11... | collective-permute-start | bytes 7077896 | tf_op jit(solution)/shard_map/ppermute | solution.py:59
  326.9 130.7 %collective-permute-start.82 = (bf16[8,96,1536]{2,1,0:T(8,128)(2,1)}, bf16[8,96,1536]{2,1,0:T(8,128)(2,1)}, u32[]{:S(2)}, u32[]{:S(2)}) collective-permute-start(bf16[8,96,1536]{2,1,0:T(8,128)(2,1)} %bitcast.561), channel_id=1, source_target_pairs={{0,1},{1,0},{2,3},{3,2},{4,5},{5,4},{6,7},{7,6},{8,9},{9,8},{10,11... | collective-permute-start | bytes 7077896 | tf_op jit(solution)/shard_map/ppermute | solution.py:59
  367.4 45.0 %collective-permute-start.75 = (bf16[8,96,384]{2,1,0:T(8,128)(2,1)S(1)}, bf16[8,96,384]{2,1,0:T(8,128)(2,1)S(1)}, u32[]{:S(2)}, u32[]{:S(2)}) collective-permute-start(bf16[8,96,384]{2,1,0:T(8,128)(2,1)S(1)} %bitcast.514), channel_id=1, source_target_pairs={{0,1},{1,0},{2,3},{3,2},{4,5},{5,4},{6,7},{7,6},{8,9},{9,8},{10,11... | collective-permute-start | bytes 1769480 | tf_op jit(solution)/shard_map/ppermute | solution.py:59
  434.1 114.2 %collective-permute-start.51 = (f32[2,1536,256]{2,1,0:T(8,128)}, f32[2,1536,256]{2,1,0:T(8,128)}, u32[]{:S(2)}, u32[]{:S(2)}) collective-permute-start(f32[2,1536,256]{2,1,0:T(8,128)} %slice.310), channel_id=1, source_target_pairs={{0,1},{1,0},{2,3},{3,2},{4,5},{5,4},{6,7},{7,6},{8,9},{9,8},{10,11... | collective-permute-start | bytes 9437192 | tf_op jit(solution)/shard_map/ppermute | solution.py:59
  436.8 76.2 %collective-permute-start.59 = (f32[2,1536,256]{2,1,0:T(8,128)}, f32[2,1536,256]{2,1,0:T(8,128)}, u32[]{:S(2)}, u32[]{:S(2)}) collective-permute-start(f32[2,1536,256]{2,1,0:T(8,128)} %slice.320), channel_id=1, source_target_pairs={{0,1},{1,0},{2,3},{3,2},{4,5},{5,4},{6,7},{7,6},{8,9},{9,8},{10,11... | collective-permute-start | bytes 9437192 | tf_op jit(solution)/shard_map/ppermute | solution.py:59
  456.7 42.5 %collective-permute-start.91 = (bf16[2,192,768]{2,1,0:T(8,128)(2,1)S(1)}, bf16[2,192,768]{2,1,0:T(8,128)(2,1)}, u32[]{:S(2)}, u32[]{:S(2)}) collective-permute-start(bf16[2,192,768]{2,1,0:T(8,128)(2,1)S(1)} %get-tuple-element.198), channel_id=1, source_target_pairs={{0,16},{4,20},{8,24},{12,28},{16,0},{20,4},{24,8},{28,12},{1,17},{... | collective-permute-start | bytes 1769480 | tf_op jit(solution)/shard_map/ppermute | solution.py:59
  457.6 41.5 %collective-permute-start.92 = (bf16[2,192,768]{2,1,0:T(8,128)(2,1)S(1)}, bf16[2,192,768]{2,1,0:T(8,128)(2,1)}, u32[]{:S(2)}, u32[]{:S(2)}) collective-permute-start(bf16[2,192,768]{2,1,0:T(8,128)(2,1)S(1)} %get-tuple-element.199), channel_id=1, source_target_pairs={{0,24},{4,28},{8,16},{12,20},{16,8},{20,12},{24,0},{28,4},{1,25},{... | collective-permute-start | bytes 1769480 | tf_op jit(solution)/shard_map/ppermute | solution.py:59
  511.1 63.9 %collective-permute-start.94 = (bf16[192,768]{1,0:T(8,128)(2,1)S(1)}, bf16[192,768]{1,0:T(8,128)(2,1)S(1)}, u32[]{:S(2)}, u32[]{:S(2)}) collective-permute-start(bf16[192,768]{1,0:T(8,128)(2,1)S(1)} %fusion.74), channel_id=1, source_target_pairs={{0,2},{1,3},{2,0},{3,1},{4,6},{5,7},{6,4},{7,5},{8,10},{9,11},{10,... | collective-permute-start | bytes 884744 | tf_op jit(solution)/shard_map/ppermute | solution.py:59
  517.3 68.8 %collective-permute-start.60 = (bf16[1536,256]{1,0:T(8,128)(2,1)}, bf16[1536,256]{1,0:T(8,128)(2,1)}, u32[]{:S(2)}, u32[]{:S(2)}) collective-permute-start(bf16[1536,256]{1,0:T(8,128)(2,1)} %get-tuple-element.203), channel_id=1, source_target_pairs={{0,2},{1,3},{2,0},{3,1},{4,6},{5,7},{6,4},{7,5},{8,10},{9,11},{10,... | collective-permute-start | bytes 2359304 | tf_op jit(solution)/shard_map/ppermute | solution.py:59
  575.0 77.0 %collective-permute-start.95 = (f32[192,768]{1,0:T(8,128)S(1)}, f32[192,768]{1,0:T(8,128)}, u32[]{:S(2)}, u32[]{:S(2)}) collective-permute-start(f32[192,768]{1,0:T(8,128)S(1)} %convert_add_fusion.6), channel_id=1, source_target_pairs={{0,1},{1,0},{2,3},{3,2},{4,5},{5,4},{6,7},{7,6},{8,9},{9,8},{10,11... | collective-permute-start | bytes 1769480 | tf_op jit(solution)/shard_map/ppermute | solution.py:59
  582.8 75.0 %collective-permute-start.88 = (f32[96,1536]{1,0:T(8,128)}, f32[96,1536]{1,0:T(8,128)}, u32[]{:S(2)}, u32[]{:S(2)}) collective-permute-start(f32[96,1536]{1,0:T(8,128)} %convert_add_fusion.7), channel_id=1, source_target_pairs={{0,1},{1,0},{2,3},{3,2},{4,5},{5,4},{6,7},{7,6},{8,9},{9,8},{10,11... | collective-permute-start | bytes 1769480 | tf_op jit(solution)/shard_map/ppermute | solution.py:59
  657.8 51.1 %collective-permute-start.103 = (f32[16,128]{1,0:T(8,128)S(1)}, f32[16,128]{1,0:T(8,128)S(1)}, u32[]{:S(2)}, u32[]{:S(2)}) collective-permute-start(f32[16,128]{1,0:T(8,128)S(1)} %add.540), channel_id=1, source_target_pairs={{0,16},{4,20},{8,24},{12,28},{16,0},{20,4},{24,8},{28,12},{1,17},{... | collective-permute-start | bytes 24584 | tf_op jit(solution)/shard_map/ppermute | solution.py:59
  (222 other events, 2813.3 us)
Sparse Core Ops, SparseCore 0:
  87.4 38.7 all-gather.3
  129.0 50.8 all-gather.5
  189.1 49.1 all-gather.7

commit v2 on v1

v2 whole, which is shorter than its diff:
```python
from functools import partial
import math

import jax
import jax.numpy as jnp
from jax import lax
from jax.experimental import pallas as pl
from jax.experimental.pallas import tpu as pltpu
from jax.sharding import PartitionSpec as P

STEP = 10

NORM_EPS = 1e-06
BETA = 0.5
ADAM_EPS = 1e-08
DECAY = 0.01
EMA_KEEP = 0.8
CLIP = 1.0

BF = jnp.bfloat16
F32 = jnp.float32
ROWS = 128
KEYS = 256
GROUP = 16
LANES = 128
FLOPS = (60 * 10**9, 10**9)
SIDE = {1: 4, 2: 4, 3: 2, 4: 2}
NT = (((1,), (1,)), ((), ()))
NN = (((1,), (0,)), ((), ()))
TN = (((0,), (0,)), ((), ()))


def dot(left, right, dims=NN):
    return lax.dot_general(left, right, dims, preferred_element_type=F32)


def inverse_rms(values):
    return lax.rsqrt(jnp.mean(values * values, axis=-1, keepdims=True) + NORM_EPS)


def rms_backward(scale_inv, normed, grad_normed):
    return scale_inv * (
        grad_normed - normed * jnp.mean(normed * grad_normed, axis=-1, keepdims=True)
    )


def adamw(weight, first, second, average, grad, rate):
    first_new = BETA * first + (1.0 - BETA) * grad
    second_new = BETA * second + (1.0 - BETA) * grad * grad
    fix = 1.0 - BETA**STEP
    weight_new = weight - rate * (
        first_new / fix / (jnp.sqrt(second_new / fix) + ADAM_EPS) + DECAY * weight
    )
    average_new = EMA_KEEP * average + (1.0 - EMA_KEEP) * weight_new
    return (first_new, second_new, weight_new, average_new)


def swap(value, axis, mask):
    size = lax.axis_size(axis)
    return lax.ppermute(value, axis, [(i, i ^ mask) for i in range(size)])


def digits_of(size):
    found = []
    stride = 1
    while stride < size:
        radix = 2 if stride == 1 or size // stride < 4 else 4
        found.append((stride, radix))
        stride *= radix
    return found


def gather_steps(size):
    steps = []
    while size > 1:
        size //= 2
        steps.append(size)
    return steps


def own_order(shards, axis):
    size = shards.shape[0]
    order = jnp.bitwise_xor(jnp.arange(size, dtype=jnp.int32), lax.axis_index(axis))
    return shards.at[order].get(mode="promise_in_bounds")


def join_pieces(pieces, axis):
    place = {}
    for _, offs in pieces:
        for off in offs:
            place[off] = len(place)
    spots = jnp.array([place[off] for off in range(len(place))], jnp.int32)
    order = jnp.bitwise_xor(jnp.arange(len(place), dtype=jnp.int32), lax.axis_index(axis))
    whole = jnp.concatenate([piece for piece, _ in pieces])
    return whole.at[spots.at[order].get(mode="promise_in_bounds")].get(mode="promise_in_bounds")


def split_blocks(blocks, axis, digits, digit):
    stride, radix = digit
    place = digits.index(digit)
    mine = (lax.axis_index(axis) // stride) % radix
    parts = [
        lax.dynamic_index_in_dim(blocks, jnp.bitwise_xor(mine, k), place, False)
        for k in range(radix)
    ]
    return parts, [d for d in digits if d != digit]


def join_blocks(parts, axis, digit, *first):
    stride, radix = digit
    got = tuple(swap(parts[k], axis, k * stride) for k in range(1, radix))
    if first:
        got = after(got, *first)
    total = parts[0].astype(F32)
    for part in got:
        total = total + part.astype(F32)
    return total


def sum_everywhere(value, axis):
    size = lax.axis_size(axis)
    stride = 1
    while stride < size:
        radix = min(8, size // stride)
        parts = [value] + [swap(value, axis, k * stride) for k in range(1, radix)]
        while len(parts) > 1:
            parts = [parts[i] + parts[i + 1] for i in range(0, len(parts), 2)]
        value = parts[0]
        stride *= radix
    return value


def after(value, *first):
    return lax.optimization_barrier((value,) + first)[0]


def spread_kernel(mixes, pre, post, pre_back, post_back):
    heads = mixes.shape[1]
    tall = heads * GROUP
    wide = (lax.broadcasted_iota(jnp.int32, (tall, heads), 0) // GROUP) == (
        lax.broadcasted_iota(jnp.int32, (tall, heads), 1)
    )
    wide = wide.astype(F32)
    row = lax.broadcasted_iota(jnp.int32, (tall, tall), 0)
    col = lax.broadcasted_iota(jnp.int32, (tall, tall), 1)
    same = row % GROUP == col % GROUP

    def exact(left, right, dims):
        return lax.dot_general(
            left, right, dims, precision=lax.Precision.HIGHEST, preferred_element_type=F32
        )

    for which, (turned, straight) in enumerate(((pre, pre_back), (post, post_back))):
        matrix = mixes[which]
        for out, dims in ((straight, NN), (turned, NT)):
            tallest = exact(wide, matrix, dims)
            full = jnp.where(same, exact(tallest, wide, NT), 0.0)
            high = full.astype(BF)
            out[:tall, :] = high
            out[tall:, :] = (full - high.astype(F32)).astype(BF)


def spread(mixes):
    tall = mixes.shape[1] * GROUP
    return pl.pallas_call(
        spread_kernel,
        out_shape=[jax.ShapeDtypeStruct((2 * tall, tall), BF)] * 4,
        name="spread",
    )(mixes)


def two_heads(rows, first, second):
    return jnp.concatenate([rows * first, rows * second], 0)


def mix(matrix, values):
    out = dot(matrix, values)
    half = matrix.shape[0] // 2
    return out[:half] + out[half:]


def head_masks(scaling):
    lane = lax.broadcasted_iota(jnp.int32, (1, LANES), 1)
    low = lane < LANES // 2
    return low, jnp.where(low, scaling, 0.0).astype(BF), jnp.where(low, 0.0, scaling).astype(BF)


def fill_sequence(meta, sources, qkv, sems):
    copies = []
    for d, source in enumerate(sources):
        start = pl.multiple_of(jnp.bitwise_xor(meta[1], d) * KEYS, KEYS)
        copies.append(pltpu.make_async_copy(source, qkv.at[pl.ds(start, KEYS)], sems.at[d]))
    for copy in copies:
        copy.start()
    for copy in copies:
        copy.wait()


def forward_kernel(meta, *refs):
    sources, (pre, post, attended, probs, weights, qkv, held, sems) = refs[:4], refs[4:]
    heads = probs.shape[0]
    width = attended.shape[1]
    pairs = heads // 2
    tall = heads * GROUP
    step = pl.program_id(0)
    pl.when(step == 0)(partial(fill_sequence, meta, sources, qkv, sems))
    length = meta[0]
    row0 = pl.multiple_of(step * KEYS + meta[2] * ROWS, ROWS)
    chunks = (jnp.minimum(row0 + ROWS, length) + KEYS - 1) // KEYS
    low, first_s, second_s = head_masks(1.0 / math.sqrt(width // heads))

    def score(kc, carry):
        k0 = pl.multiple_of(kc * KEYS, KEYS)
        for p in range(pairs):
            at = p * LANES
            queries = two_heads(qkv[pl.ds(row0, ROWS), at : at + LANES], first_s, second_s)
            keys = qkv[pl.ds(k0, KEYS), width + at : width + at + LANES]
            scores = dot(queries, keys, NT).astype(BF)
            weights[2 * p : 2 * p + 2, :, pl.ds(k0, KEYS)] = scores.reshape(2, ROWS, KEYS)
        return carry

    lax.fori_loop(0, chunks, score, 0)

    def group(n, batch, carry):
        side = SIDE[n]
        rows = [
            pl.ds(pl.multiple_of((batch * side + u) * GROUP, GROUP), GROUP) for u in range(side)
        ]
        col_at = lax.broadcasted_iota(jnp.int32, (GROUP, KEYS), 1)
        row_at = lax.broadcasted_iota(jnp.int32, (GROUP, KEYS), 0)
        peak = [None] * side
        total = [None] * side
        for kc in range(n):
            cols = slice(kc * KEYS, (kc + 1) * KEYS)
            for u in range(side):
                mixed = mix(pre[...], weights[:, rows[u], cols].reshape(tall, KEYS))
                key_pos = col_at + kc * KEYS
                query_pos = row0 + (batch * side + u) * GROUP + row_at
                allowed = (key_pos <= query_pos) & (key_pos < length)
                mixed = jnp.where(allowed[None], mixed.reshape(heads, GROUP, KEYS), -1e30)
                mixed = mixed.reshape(tall, KEYS)
                held[u, :, cols] = mixed
                part = jnp.maximum(mixed[:, :LANES], mixed[:, LANES:])
                peak[u] = part if kc == 0 else jnp.maximum(peak[u], part)
        top = [jnp.max(peak[u], axis=1, keepdims=True) for u in range(side)]
        for kc in range(n):
            cols = slice(kc * KEYS, (kc + 1) * KEYS)
            for u in range(side):
                shifted = jnp.exp(held[u, :, cols] - top[u])
                held[u, :, cols] = shifted
                part = shifted[:, :LANES] + shifted[:, LANES:]
                total[u] = part if kc == 0 else total[u] + part
        inverse = [1.0 / jnp.sum(total[u], axis=1, keepdims=True) for u in range(side)]
        for kc in range(n):
            cols = slice(kc * KEYS, (kc + 1) * KEYS)
            for u in range(side):
                low_probs = (held[u, :, cols] * inverse[u]).astype(BF)
                probs[:, rows[u], cols] = low_probs.reshape(heads, GROUP, KEYS)
                mixed = mix(post[...], low_probs).astype(BF)
                weights[:, rows[u], cols] = mixed.reshape(heads, GROUP, KEYS)
        return carry

    def rest(n):
        lax.fori_loop(0, ROWS // GROUP // SIDE[n], partial(group, n), 0)
        for p in range(pairs):
            at = p * LANES
            pair = weights[2 * p : 2 * p + 2, :, : n * KEYS].reshape(2 * ROWS, n * KEYS)
            out = dot(pair, qkv[: n * KEYS, 2 * width + at : 2 * width + at + LANES])
            attended[:, at : at + LANES] = jnp.where(low, out[:ROWS], out[ROWS:]).astype(BF)

    for n in range(1, probs.shape[2] // KEYS + 1):
        pl.when(chunks == n)(partial(rest, n))


def backward_kernel(meta, *refs):
    sources, refs = refs[:4], refs[4:]
    grad_rows, pre, post, probs, weights, stay, away, grad_pre, grad_post = refs[:9]
    qkv, scores, grads, held, grad_qkv, sum_pre, sum_post, sems = refs[9:]
    heads = probs.shape[0]
    width = grad_rows.shape[1]
    pairs = heads // 2
    tall = heads * GROUP
    step = pl.program_id(0)
    me = meta[1]

    @pl.when(step == 0)
    def _():
        grad_qkv[...] = jnp.zeros_like(grad_qkv)
        sum_pre[...] = jnp.zeros_like(sum_pre)
        sum_post[...] = jnp.zeros_like(sum_post)
        fill_sequence(meta, sources, qkv, sems)

    length = meta[0]
    row0 = pl.multiple_of(step * KEYS + meta[2] * ROWS, ROWS)
    chunks = (jnp.minimum(row0 + ROWS, length) + KEYS - 1) // KEYS
    chunks = jnp.where(row0 < length, chunks, 0)
    scaling = 1.0 / math.sqrt(width // heads)
    low, first_s, second_s = head_masks(scaling)
    low, first_one, second_one = head_masks(1.0)
    lanes = pl.ds(pl.multiple_of(meta[2] * ROWS, ROWS), ROWS)

    def slot_of(home):
        d = jnp.bitwise_xor(me, home)
        return 2 * jnp.bitwise_and(d, 1) + d // 2


    def score(kc, carry):
        k0 = pl.multiple_of(kc * KEYS, KEYS)
        for p in range(pairs):
            at = p * LANES
            queries = two_heads(qkv[pl.ds(row0, ROWS), at : at + LANES], first_s, second_s)
            grad = two_heads(grad_rows[:, at : at + LANES], first_one, second_one)
            keys = qkv[pl.ds(k0, KEYS), width + at : width + at + LANES]
            values = qkv[pl.ds(k0, KEYS), 2 * width + at : 2 * width + at + LANES]
            both = slice(2 * p, 2 * p + 2)
            cols = pl.ds(k0, KEYS)
            scores[both, :, cols] = dot(queries, keys, NT).astype(BF).reshape(2, ROWS, KEYS)
            grads[both, :, cols] = dot(grad, values, NT).astype(BF).reshape(2, ROWS, KEYS)
        return carry

    lax.fori_loop(0, chunks, score, 0)

    def group(n, batch, carry):
        side = SIDE[n]
        rows = [
            pl.ds(pl.multiple_of((batch * side + u) * GROUP, GROUP), GROUP) for u in range(side)
        ]
        span = slice(0, n * KEYS)
        total = [None] * side
        for kc in range(n):
            cols = slice(kc * KEYS, (kc + 1) * KEYS)
            for u in range(side):
                grad_probs = mix(post[...], grads[:, rows[u], cols].reshape(tall, KEYS))
                held[u, :, cols] = grad_probs
                term = probs[:, rows[u], cols].reshape(tall, KEYS).astype(F32) * grad_probs
                part = term[:, :LANES] + term[:, LANES:]
                total[u] = part if kc == 0 else total[u] + part
        added = None
        for u in range(side):
            left = probs[:, rows[u], span].reshape(tall, n * KEYS)
            term = dot(left, grads[:, rows[u], span].reshape(tall, n * KEYS), NT)
            added = term if u == 0 else added + term
        sum_post[...] += added
        delta = [jnp.sum(total[u], axis=1, keepdims=True) for u in range(side)]
        mixed = [[] for _ in range(side)]
        for kc in range(n):
            cols = slice(kc * KEYS, (kc + 1) * KEYS)
            for u in range(side):
                prob = probs[:, rows[u], cols].reshape(tall, KEYS).astype(F32)
                grad_mixed = (prob * (held[u, :, cols] - delta[u])).astype(BF)
                mixed[u].append(grad_mixed)
                back = mix(pre[...], grad_mixed).astype(BF)
                grads[:, rows[u], cols] = back.reshape(heads, GROUP, KEYS)
        added = None
        for u in range(side):
            left = scores[:, rows[u], span].reshape(tall, n * KEYS)
            term = dot(left, jnp.concatenate(mixed[u], 1), NT)
            added = term if u == 0 else added + term
        sum_pre[...] += added
        return carry

    def rest(n):
        lax.fori_loop(0, ROWS // GROUP // SIDE[n], partial(group, n), 0)
        for p in range(pairs):
            at = p * LANES
            mine = slice(at, at + LANES)
            both = slice(2 * p, 2 * p + 2)
            queries = two_heads(qkv[pl.ds(row0, ROWS), mine], first_s, second_s).T
            grad = two_heads(grad_rows[:, mine], first_one, second_one).T
            back = grads[both, :, : n * KEYS].reshape(2 * ROWS, n * KEYS)
            out = dot(back, qkv[: n * KEYS, width + at : width + at + LANES])
            out = jnp.where(low, out[:ROWS], out[ROWS:]) * scaling
            grad_qkv[slot_of(step), mine, lanes] = out.T
            for kc in range(n):
                cols = slice(kc * KEYS, (kc + 1) * KEYS)
                to = slot_of(kc)
                grad_qkv[to, width + at : width + at + LANES, :] += dot(
                    queries, grads[both, :, cols].reshape(2 * ROWS, KEYS)
                )
                grad_qkv[to, 2 * width + at : 2 * width + at + LANES, :] += dot(
                    grad, weights[both, :, cols].reshape(2 * ROWS, KEYS)
                )

    for n in range(1, probs.shape[2] // KEYS + 1):
        pl.when(chunks == n)(partial(rest, n))

    @pl.when(step == pl.num_programs(0) - 1)
    def _():
        stay[...] = grad_qkv[:2]
        away[...] = grad_qkv[2:].astype(BF)
        row = lax.broadcasted_iota(jnp.int32, (tall, tall), 0)
        col = lax.broadcasted_iota(jnp.int32, (tall, tall), 1)
        same = row % GROUP == col % GROUP
        pick = (
            lax.broadcasted_iota(jnp.int32, (tall, LANES), 0) // GROUP
            == lax.broadcasted_iota(jnp.int32, (tall, LANES), 1)
        ).astype(F32)
        for source, out in ((sum_pre, grad_pre), (sum_post, grad_post)):
            kept = jnp.where(same, source[...], 0.0)
            wide = lax.dot_general(
                kept, pick, NN, precision=lax.Precision.HIGHEST, preferred_element_type=F32
            )
            for head in range(heads):
                out[head : head + 1, :] = jnp.sum(
                    wide[head * GROUP : (head + 1) * GROUP], axis=0, keepdims=True
                )


ANY = pl.BlockSpec(memory_space=pl.ANY)


def is_live(step, meta):
    return step * KEYS + meta[2] * ROWS < meta[0]


def attend(meta, sources, pre, post, heads, flops):
    width = sources[0].shape[1] // 3
    tall = heads * GROUP
    steps = 4
    full_len = steps * KEYS
    matrix = pl.BlockSpec((2 * tall, tall), lambda i, m: (0, 0), pipeline_mode=pl.Buffered(1))
    wide = pl.BlockSpec(
        (None, heads, ROWS, full_len), lambda i, m: (jnp.where(is_live(i, m), i, steps), 0, 0, 0)
    )
    kept = jax.ShapeDtypeStruct((steps + 1, heads, ROWS, full_len), BF)
    return pl.pallas_call(
        forward_kernel,
        grid_spec=pltpu.PrefetchScalarGridSpec(
            num_scalar_prefetch=1,
            grid=(steps,),
            in_specs=[ANY] * 4 + [matrix, matrix],
            out_specs=[
                pl.BlockSpec((None, ROWS, width), lambda i, m: (jnp.bitwise_xor(i, m[1]), 0, 0)),
                wide,
                wide,
            ],
            scratch_shapes=[
                pltpu.VMEM((full_len, 3 * width), BF),
                pltpu.VMEM((4, tall, full_len), F32),
                pltpu.SemaphoreType.DMA((4,)),
            ],
        ),
        out_shape=[jax.ShapeDtypeStruct((steps, ROWS, width), BF), kept, kept],
        compiler_params=pltpu.CompilerParams(vmem_limit_bytes=56 * 2**20),
        cost_estimate=pl.CostEstimate(
            flops=flops, bytes_accessed=2**20, transcendentals=0
        ),
        name="attend",
    )(meta, *sources, pre, post)


def attend_back(meta, sources, grad_rows, pre, post, probs, weights, flops):
    width = sources[0].shape[1] // 3
    steps = 4
    heads = probs.shape[1]
    tall = heads * GROUP
    full_len = steps * KEYS

    def newest(step, meta):
        last = 0
        for other in range(1, steps):
            last = jnp.where(is_live(other, meta), other, last)
        return jnp.minimum(step, last)

    matrix = pl.BlockSpec((2 * tall, tall), lambda i, m: (0, 0), pipeline_mode=pl.Buffered(1))
    wide = pl.BlockSpec((None, heads, ROWS, full_len), lambda i, m: (newest(i, m), 0, 0, 0))
    rows = pl.BlockSpec((None, ROWS, width), lambda i, m: (jnp.bitwise_xor(i, m[1]), 0, 0))
    small = pl.BlockSpec((heads, LANES), lambda i, m: (0, 0))
    pairs = pl.BlockSpec(
        (2, 3 * width, KEYS), lambda i, m: (0, 0, 0), pipeline_mode=pl.Buffered(1)
    )
    return pl.pallas_call(
        backward_kernel,
        grid_spec=pltpu.PrefetchScalarGridSpec(
            num_scalar_prefetch=1,
            grid=(steps,),
            in_specs=[ANY] * 4 + [rows, matrix, matrix, wide, wide],
            out_specs=[
                pairs,
                pairs,
                small,
                small,
            ],
            scratch_shapes=[
                pltpu.VMEM((full_len, 3 * width), BF),
                pltpu.VMEM((heads, ROWS, full_len), BF),
                pltpu.VMEM((heads, ROWS, full_len), BF),
                pltpu.VMEM((4, tall, full_len), F32),
                pltpu.VMEM((4, 3 * width, KEYS), F32),
                pltpu.VMEM((tall, tall), F32),
                pltpu.VMEM((tall, tall), F32),
                pltpu.SemaphoreType.DMA((4,)),
            ],
        ),
        out_shape=[
            jax.ShapeDtypeStruct((2, 3 * width, KEYS), F32),
            jax.ShapeDtypeStruct((2, 3 * width, KEYS), BF),
            jax.ShapeDtypeStruct((heads, LANES), F32),
            jax.ShapeDtypeStruct((heads, LANES), F32),
        ],
        compiler_params=pltpu.CompilerParams(vmem_limit_bytes=60 * 2**20),
        cost_estimate=pl.CostEstimate(
            flops=flops, bytes_accessed=2**20, transcendentals=0
        ),
        name="attend_back",
    )(meta, *sources, grad_rows, pre, post, probs, weights)


def gelu_both(value):
    scale = math.sqrt(2.0 / math.pi)
    square = value * value
    bent = jnp.tanh(scale * (value + 0.044715 * (square * value)))
    share = 0.5 * (1.0 + bent)
    slope = share + 0.5 * value * (1.0 - bent * bent) * (
        scale * (1.0 + 3.0 * 0.044715 * square)
    )
    return value * share, slope


def fill_weights(meta, sources, offs, inner, outer, proj, sems):
    hidden = inner.shape[1] // 2
    width = proj.shape[0]
    half = width // 2
    copies = []

    def copy(source, target):
        copies.append(pltpu.make_async_copy(source, target, sems.at[len(copies)]))

    count = len(sources) // 2
    for side in range(2):
        lanes = jnp.bitwise_xor(meta[1], side) * half
        to_proj = pl.ds(pl.multiple_of(lanes, LANES), half)
        to_inner = slice(side * hidden, (side + 1) * hidden)
        here = sources[count * side : count * side + count]
        if offs is None:
            copy(here[0], inner.at[:, to_inner])
            copy(here[1], proj.at[:, to_proj])
            copy(here[2], outer.at[to_inner])
            continue
        own_rows = here[0].shape[1]
        folds = hidden * own_rows // width // own_rows
        for source, owners in zip(here, offs):
            for at_source, off in enumerate(owners):
                block = source.at[at_source]
                owner = jnp.bitwise_xor(meta[0], off)
                rows = pl.ds(pl.multiple_of(owner * own_rows, own_rows), own_rows)
                copy(block.at[:, :hidden], inner.at[rows, to_inner])
                copy(block.at[:, hidden : hidden + half], proj.at[rows, to_proj])
                for fold in range(folds):
                    start = side * hidden + (owner * folds + fold) * own_rows
                    at = hidden + half + fold * width
                    copy(
                        block.at[:, at : at + width],
                        outer.at[pl.ds(pl.multiple_of(start, own_rows), own_rows)],
                    )
    for one in copies:
        one.start()
    for one in copies:
        one.wait()


TILE = 256
CHUNK = 512


def feed_kernel(offs, meta, gains, tokens, attended, grad_out, *refs):
    count = len(refs) - 17
    sources, refs = refs[:count], refs[count:]
    output, grad_resid, resid_low, grad_attended, gain_two, second_in = refs[:6]
    active, grad_hidden = refs[6:8], refs[8:10]
    inner, outer, proj, resid, out_sum, grad_sum, sems = refs[10:]
    rows = tokens.shape[0]
    step = pl.program_id(0)
    tiles = [slice(at, at + TILE) for at in range(0, rows, TILE)]

    @pl.when(step == 0)
    def _():
        fill_weights(meta, sources, offs, inner, outer, proj, sems)
        for tile in tiles:
            value = tokens[tile].astype(F32) + dot(attended[tile], proj[...])
            resid[tile] = value
            out_sum[tile] = value
            grad_sum[tile] = jnp.zeros_like(value)
            second_in[tile] = (value * inverse_rms(value) * gains[1:2]).astype(BF)

    cols = pl.ds(pl.multiple_of(step * CHUNK, CHUNK), CHUNK)
    for tile in tiles:
        up = inner[:, cols]
        down = outer[cols]
        value, slope = gelu_both(dot(second_in[tile], up))
        value = value.astype(BF)
        back = (dot(grad_out[tile], down, NT) * slope).astype(BF)
        for side in range(2):

            @pl.when((step * 2 >= pl.num_programs(0)) == (side == 1))
            def _():
                active[side][tile] = value
                grad_hidden[side][tile] = back

        out_sum[tile] += dot(value, down)
        grad_sum[tile] += dot(back, up, NT)

    @pl.when(step == pl.num_programs(0) - 1)
    def _():
        gain_sum = jnp.zeros((8, proj.shape[0]), F32)
        for tile in tiles:
            output[tile] = out_sum[tile].astype(BF)
            value = resid[tile]
            scale = inverse_rms(value)
            normed = value * scale
            grad = grad_sum[tile]
            gain_sum += jnp.sum((grad * normed).reshape(TILE // 8, 8, -1), axis=0)
            back = grad_out[tile].astype(F32) + rms_backward(scale, normed, grad * gains[1:2])
            grad_resid[tile] = back
            back = back.astype(BF)
            resid_low[tile] = back
            grad_attended[tile] = dot(back, proj[...], NT).astype(BF)
        gain_two[...] = gain_sum


def feed_forward(meta, gains, tokens, attended, grad_out, sources, offs, hidden):
    rows, width = tokens.shape
    copies = 6
    if offs is not None:
        owners = sum(len(o) for o in offs)
        copies = 2 * owners * (2 + hidden // 2 // width)
    chunks = hidden // CHUNK

    def whole(shape):
        return pl.BlockSpec(shape, lambda c, m: (0,) * len(shape), pipeline_mode=pl.Buffered(1))

    flat = whole((rows, width))
    first = pl.BlockSpec((rows, CHUNK), lambda c, m: (0, jnp.minimum(c, chunks // 2 - 1)))
    second = pl.BlockSpec((rows, CHUNK), lambda c, m: (0, jnp.maximum(c - chunks // 2, 0)))
    wide = jax.ShapeDtypeStruct((rows, hidden // 2), BF)
    return pl.pallas_call(
        partial(feed_kernel, offs),
        grid_spec=pltpu.PrefetchScalarGridSpec(
            num_scalar_prefetch=1,
            grid=(chunks,),
            in_specs=[whole((2, width)), flat, flat, flat] + [ANY] * len(sources),
            out_specs=[flat, flat, flat, flat, whole((8, width)), flat, first, second, first, second],
            scratch_shapes=[
                pltpu.VMEM((width, hidden), BF),
                pltpu.VMEM((hidden, width), BF),
                pltpu.VMEM((width, width), BF),
                pltpu.VMEM((rows, width), F32),
                pltpu.VMEM((rows, width), F32),
                pltpu.VMEM((rows, width), F32),
                pltpu.SemaphoreType.DMA((copies,)),
            ],
        ),
        out_shape=[
            jax.ShapeDtypeStruct((rows, width), BF),
            jax.ShapeDtypeStruct((rows, width), F32),
            jax.ShapeDtypeStruct((rows, width), BF),
            jax.ShapeDtypeStruct((rows, width), BF),
            jax.ShapeDtypeStruct((8, width), F32),
            jax.ShapeDtypeStruct((rows, width), BF),
            wide,
            wide,
            wide,
            wide,
        ],
        compiler_params=pltpu.CompilerParams(vmem_limit_bytes=56 * 2**20),
        cost_estimate=pl.CostEstimate(
            flops=22 * 10**9, bytes_accessed=40 * 10**6, transcendentals=0
        ),
        name="feed_forward",
    )(meta, gains, tokens, attended, grad_out, *sources)


def weight_kernel(meta, second_in, attended, resid_low, grad_out, active, back, first, last, turned):
    width = second_in.shape[1]
    hidden = active.shape[1]
    half = width // 2
    turned[...] = second_in[...].T
    lanes = pl.ds(pl.multiple_of(meta[0] * half, LANES), half)
    first[:, hidden:] = dot(attended[...], resid_low[:, lanes], TN).astype(first.dtype)
    for at in range(0, hidden, CHUNK):
        cols = slice(at, at + CHUNK)
        first[:, cols] = dot(turned[...], back[:, cols]).astype(first.dtype)
        last[cols] = dot(active[:, cols], grad_out[...], TN).astype(last.dtype)


def weight_sums(which, second_in, attended, resid_low, grad_out, active, back, kind):
    rows, width = second_in.shape
    hidden = active.shape[1]
    vmem = pl.BlockSpec(memory_space=pltpu.VMEM)
    return pl.pallas_call(
        weight_kernel,
        in_specs=[pl.BlockSpec(memory_space=pltpu.SMEM)] + [vmem] * 6,
        out_specs=[vmem, vmem],
        scratch_shapes=[pltpu.VMEM((width, rows), BF)],
        out_shape=[
            jax.ShapeDtypeStruct((width, hidden + width // 2), kind),
            jax.ShapeDtypeStruct((hidden, width), kind),
        ],
        compiler_params=pltpu.CompilerParams(vmem_limit_bytes=56 * 2**20),
        cost_estimate=pl.CostEstimate(
            flops=6 * 10**9, bytes_accessed=20 * 10**6, transcendentals=0
        ),
        name="weight_sums",
    )(which, second_in, attended, resid_low, grad_out, active, back)


def first_kernel(offs, meta, tokens, *refs):
    count = 2 * (1 if offs is None else len(offs))
    sources, refs = refs[:count], refs[count:]
    out, first_in, gains, refs = refs[0], refs[1], refs[2], refs[3:]
    weight, mixed, sems = refs
    side = weight.shape[1] // 2
    copies = []

    def copy(source, target):
        copies.append(pltpu.make_async_copy(source, target, sems.at[len(copies)]))

    for which in range(2):
        here = sources[which * (count // 2) : (which + 1) * (count // 2)]
        start = pl.multiple_of(jnp.bitwise_xor(meta[1], which) * side, side)
        if offs is None:
            copy(here[0].at[:, :side], weight.at[:, pl.ds(start, side)])
            if which == 0:
                copy(here[0].at[:, side:], mixed)
            continue
        own_rows = here[0].shape[1]
        for source, owners in zip(here, offs):
            for at, off in enumerate(owners):
                owner = jnp.bitwise_xor(meta[0], off)
                rows = pl.ds(pl.multiple_of(owner * own_rows, own_rows), own_rows)
                copy(source.at[at, :, :side], weight.at[rows, pl.ds(start, side)])
                if which == 0:
                    copy(source.at[at, :, side:], mixed.at[rows])
    for one in copies:
        one.start()
    for one in copies:
        one.wait()
    gain = mixed[...].astype(F32).T[:8]
    gains[...] = gain
    for at in range(0, tokens.shape[0], KEYS):
        value = tokens[at : at + KEYS].astype(F32)
        low = (value * inverse_rms(value) * gain[:1]).astype(BF)
        first_in[at : at + KEYS] = low
        for col in range(0, 2 * side, width_of(side)):
            cols = slice(col, col + width_of(side))
            out[at : at + KEYS, cols] = dot(low, weight[:, cols]).astype(BF)


def width_of(side):
    return 2 * side // 3


def first_product(meta, tokens, pieces, offs, with_weight):
    rows, width = tokens.shape
    vmem = pl.BlockSpec(memory_space=pltpu.VMEM)
    out_shape = [
        jax.ShapeDtypeStruct((rows, 3 * width), BF),
        jax.ShapeDtypeStruct((rows, width), BF),
        jax.ShapeDtypeStruct((8, width), F32),
    ]
    scratch = [
        pltpu.VMEM((width, LANES), BF),
        pltpu.SemaphoreType.DMA((3 if offs is None else 3 * sum(len(o) for o in offs),)),
    ]
    if with_weight:
        out_shape.append(jax.ShapeDtypeStruct((width, 3 * width), BF))
    else:
        scratch = [pltpu.VMEM((width, 3 * width), BF)] + scratch
    return pl.pallas_call(
        partial(first_kernel, offs),
        in_specs=[pl.BlockSpec(memory_space=pltpu.SMEM), vmem] + [ANY] * len(pieces),
        out_specs=[vmem] * len(out_shape),
        out_shape=out_shape,
        scratch_shapes=scratch,
        compiler_params=pltpu.CompilerParams(vmem_limit_bytes=40 * 2**20),
        cost_estimate=pl.CostEstimate(
            flops=4 * 10**9, bytes_accessed=5 * 2**20, transcendentals=0
        ),
        name="first_product",
    )(meta, tokens, *pieces)


def first_grads_kernel(meta, first_in, *refs):
    cols, (out,) = refs[:-1], refs[-1:]
    side = out.shape[1]
    take = pl.ds(pl.multiple_of(meta[0] * side, side), side)
    total = None
    for block, grads in enumerate(cols):
        rows = first_in[block * KEYS : (block + 1) * KEYS].T
        term = dot(rows, grads[take], NT)
        total = term if block == 0 else total + term
        if block + 1 < len(cols):
            continue
        out[...] = total.astype(out.dtype)


def first_grads(which, first_in, cols, kind):
    width = first_in.shape[1]
    side = cols[0].shape[0] // 2
    vmem = pl.BlockSpec(memory_space=pltpu.VMEM)
    return pl.pallas_call(
        first_grads_kernel,
        in_specs=[pl.BlockSpec(memory_space=pltpu.SMEM)] + [vmem] * (1 + len(cols)),
        out_specs=vmem,
        out_shape=jax.ShapeDtypeStruct((width, side), kind),
        compiler_params=pltpu.CompilerParams(vmem_limit_bytes=50 * 2**20),
        cost_estimate=pl.CostEstimate(
            flops=3 * 10**9, bytes_accessed=5 * 2**20, transcendentals=0
        ),
        name="first_grads",
    )(which, first_in, *cols)


def token_grads_kernel(meta, gains, near, far, weight, tokens, grad_resid, *refs):
    out, gain_out = refs[-2:]
    step = pl.program_id(0)

    @pl.when(step == 0)
    def _():
        gain_out[...] = jnp.zeros_like(gain_out)

    for which, grads in enumerate((near, far)):

        @pl.when(step == which)
        def _():
            back = dot(weight[...], grads[...]).T
            value = tokens[...].astype(F32)
            scale = inverse_rms(value)
            normed = value * scale
            gain_out[...] += jnp.sum((back * normed).reshape(KEYS // 8, 8, -1), axis=0)
            out[...] = grad_resid[...] + rms_backward(scale, normed, back * gains[:1])


def token_grads(slot, seqs, gains, near, far, weight, tokens, grad_resid, before):
    _, rows, width = tokens.shape

    def whole(shape):
        return pl.BlockSpec(shape, lambda i, m: (0,) * len(shape), pipeline_mode=pl.Buffered(1))

    place = pl.BlockSpec((None, rows, width), lambda i, m: (m[i], 0, 0))
    extra = [] if before is None else [before]
    return pl.pallas_call(
        token_grads_kernel,
        grid_spec=pltpu.PrefetchScalarGridSpec(
            num_scalar_prefetch=1,
            grid=(2,),
            in_specs=[
                whole(gains.shape),
                whole(near.shape),
                whole(far.shape),
                whole(weight.shape),
                place,
                pl.BlockSpec((None, rows, width), lambda i, m: (2 * slot + i, 0, 0)),
            ]
            + [ANY] * len(extra),
            out_specs=[place, whole((8, width))],
        ),
        out_shape=[
            jax.ShapeDtypeStruct(tokens.shape, F32),
            jax.ShapeDtypeStruct((8, width), F32),
        ],
        input_output_aliases={7: 0} if extra else {},
        compiler_params=pltpu.CompilerParams(vmem_limit_bytes=50 * 2**20),
        cost_estimate=pl.CostEstimate(
            flops=4 * 10**9, bytes_accessed=5 * 2**20, transcendentals=0
        ),
        name="token_grads",
    )(seqs, gains, near, far, weight, tokens, grad_resid, *extra)


def on_device(
    tokens,
    cotangent,
    lengths,
    qkv_weight,
    qkv_first,
    qkv_second,
    qkv_average,
    proj_weight,
    proj_first,
    proj_second,
    proj_average,
    inner_weight,
    inner_first,
    inner_second,
    inner_average,
    outer_weight,
    outer_first,
    outer_second,
    outer_average,
    gains,
    gain_first,
    gain_second,
    gain_average,
    mixes,
    mix_first,
    mix_second,
    mix_average,
):
    group_seqs, shard_len, width = tokens.shape
    owners = lax.axis_size("dp")
    heads = mixes.shape[1]
    own_rows = qkv_weight.shape[0]
    hidden = inner_weight.shape[1]
    half = width // 2
    slice_ff = hidden // owners // 2
    me = lax.axis_index("seq")
    pair = me // 2
    core = jnp.bitwise_and(me, 1)

    def by_core(mine, other, axis):
        return jnp.where(
            core == 0,
            jnp.concatenate([mine, other], axis),
            jnp.concatenate([other, mine], axis),
        )

    ahead = (lengths[None, :] > lengths[:, None]) | (
        (lengths[None, :] == lengths[:, None])
        & (jnp.arange(group_seqs)[None, :] < jnp.arange(group_seqs)[:, None])
    )
    rank = jnp.sum(ahead.astype(jnp.int32), axis=1)
    order = jnp.sum(
        jnp.where(
            rank[None, :] == jnp.arange(group_seqs)[:, None], jnp.arange(group_seqs)[None, :], 0
        ),
        axis=1,
    ).astype(jnp.int32)

    def sequence_of(slot, which):
        return order[which if slot == 0 else group_seqs - 1 - which]

    def arrange(value):
        return jnp.stack(
            [
                jnp.stack(
                    [
                        lax.dynamic_index_in_dim(
                            value, sequence_of(slot, jnp.bitwise_xor(pair, d)), 0, False
                        )
                        for d in range(2)
                    ]
                )
                for slot in range(2)
            ]
        )

    def restore(value):
        flat = value.reshape((4,) + value.shape[2:])
        which = jnp.where(rank < 2, rank, 3 - rank)
        place = 2 * (rank // 2) + jnp.bitwise_xor(which, pair)
        return flat.at[place].get(mode="promise_in_bounds")

    lengths_here = arrange(lengths)
    metas = [jnp.stack([lengths_here[slot, 0], me, core]).astype(jnp.int32) for slot in range(2)]

    low_rows = arrange(tokens)
    pre_mix, post_mix, pre_back, post_back = spread(mixes)
    positions = me * shard_len + jnp.arange(shard_len, dtype=jnp.int32)
    live = positions[None, None, :] < lengths_here[:, :, None]
    cot = arrange(cotangent)
    grad_out = jnp.where(live[..., None], cot, jnp.zeros_like(cot))
    side = qkv_weight.shape[1] // 2
    mine = lax.dynamic_slice_in_dim(qkv_weight.astype(BF), core * side, side, 1)
    mine = jnp.concatenate([mine, jnp.pad(gains.astype(BF).T, ((0, 0), (0, LANES - 2)))], 1)
    offs = None
    if owners == 8:
        shard = mine[None]
        got = swap(shard, "dp", 4)
        got, early = lax.optimization_barrier((got, (low_rows, pre_mix, grad_out)))
        pieces = [jnp.concatenate([shard, got])]
        far_z, far_x = swap(pieces[0], "dp", 2), swap(pieces[0], "dp", 1)
        beside = [swap(pieces[0], "seq", 1)]
        pieces += [far_z, far_x]
        pieces.append(swap(far_z, "dp", 1))
        beside += [swap(p, "seq", 1) for p in pieces[1:]]
        offs = ((0, 4), (2, 6), (1, 5), (3, 7))
        pieces += beside
        late = pieces[3]
    else:
        mine = lax.all_gather(mine, "dp", axis=0, tiled=True)
        pieces = [mine, swap(mine, "seq", 1)]
        early = late = mine

    folds = slice_ff // own_rows
    inner_mine = inner_weight.astype(BF).reshape(own_rows, owners, 2, slice_ff)
    inner_mine = lax.dynamic_index_in_dim(inner_mine, core, 2, False)
    outer_mine = outer_weight.astype(BF).reshape(2, folds, own_rows, width)
    outer_mine = lax.dynamic_index_in_dim(outer_mine, core, 0, False)
    rest = jnp.concatenate(
        [
            inner_mine.reshape(own_rows, owners * slice_ff),
            lax.dynamic_slice_in_dim(proj_weight.astype(BF), core * half, half, 1),
        ]
        + [outer_mine[f] for f in range(folds)],
        axis=1,
    )[None]
    if offs is not None:
        got = swap(after(rest, early), "dp", 4)
        got, late = lax.optimization_barrier((got, late))
    place = jnp.stack([lax.axis_index("dp"), core]).astype(jnp.int32)
    out, *_ = first_product(place, low_rows[0, 1], pieces, offs, False)
    far = [out]
    if offs is not None:
        got = after(got, far[0])
        rest_pieces = [jnp.concatenate([rest, got])]
        far_z, far_x = swap(rest_pieces[0], "dp", 2), swap(rest_pieces[0], "dp", 1)
    here = swap(far[0], "seq", 2)
    out, first_in, gain_vals, weight_qkv = first_product(
        after(place, far[0]), low_rows.reshape(-1, width), pieces, offs, True
    )
    out = out.reshape(4, shard_len, 3 * width)
    near = [out[0], out[2]]
    far.append(out[3])
    beside = swap(near[0], "seq", 1)
    if offs is None:
        here, beside = lax.optimization_barrier((here, beside, far[1], near[1]))[:2]
    else:
        here, beside, far_z, far_x = lax.optimization_barrier(
            (here, beside, far_z, far_x, far[1], near[1])
        )[:4]
        rest_pieces += [far_z, far_x]
        far_x = swap(far_z, "dp", 1)
    sources = [[near[0], beside, here, swap(here, "seq", 1)]]
    next_far = swap(after(far[1], here), "seq", 2)
    beside = swap(after(near[1], here), "seq", 1)
    def by_half(rows):
        return jnp.where(core == 0, rows, rows[:, ::-1])

    rows, probs, weights = [None, None], [None, None], [None, None]
    meta = after(metas[0], sources[0], rest)
    if offs is not None:
        beside_rest = [swap(p, "seq", 1) for p in rest_pieces]
    rows[0], probs[0], weights[0] = attend(meta, sources[0], pre_mix, post_mix, heads, FLOPS[0])
    next_far, beside = lax.optimization_barrier((next_far, beside, rows[0]))[:2]
    if offs is not None:
        rest_pieces.append(after(far_x, rows[0]))
        beside_rest.append(swap(rest_pieces[3], "seq", 1))
    sources.append([near[1], beside, next_far, swap(next_far, "seq", 1)])
    far_rows = swap(rows[0][2:], "seq", 2)
    rows[1], probs[1], weights[1] = attend(
        metas[1], sources[1], pre_mix, post_mix, heads, FLOPS[1]
    )
    far_rows = after(far_rows, rows[1])
    cut = owners * slice_ff + half
    if offs is not None:
        beside_rest = after(beside_rest, rows[1])
        feed_weights = rest_pieces + list(beside_rest)
    else:
        rest = lax.all_gather(rest[0], "dp")
        feed_weights = []
        for part in (rest, swap(rest, "seq", 1)):
            flat = part.reshape(owners * own_rows, -1)
            down = jnp.moveaxis(part[:, :, cut:].reshape(owners, own_rows, folds, width), 2, 1)
            feed_weights += [
                flat[:, : cut - half],
                flat[:, cut - half : cut],
                down.reshape(owners * slice_ff, width),
            ]
    far_rows = jnp.stack([far_rows, swap(rows[1][2:], "seq", 2)])
    near_rows = jnp.stack([rows[0][1], rows[1][1]])
    got = swap(jnp.stack([near_rows, far_rows[:, 1]]), "seq", 1)
    attention_output = jnp.stack(
        [
            by_half(
                jnp.stack(
                    [
                        jnp.stack([rows[slot][0], got[0, slot]]),
                        jnp.stack([far_rows[slot, 0], got[1, slot]]),
                    ]
                )
            ).reshape(2, 2 * ROWS, width)
            for slot in range(2)
        ]
    )

    flat = (-1, width)
    attention_output = attention_output.reshape(flat)
    flat_out = grad_out.reshape(flat)
    output, grad_resid, resid_low, grad_attended, gain_two, second_in, *wide = feed_forward(
        place,
        gain_vals[:2],
        low_rows.reshape(flat),
        attention_output,
        flat_out,
        feed_weights,
        offs,
        hidden,
    )
    grad_attended = grad_attended.reshape(grad_out.shape)
    grad_resid = grad_resid.reshape(4, shard_len, width)

    def sums_of(side, which, kind):
        return weight_sums(
            which[None],
            second_in,
            attention_output,
            resid_low,
            flat_out,
            wide[side],
            wide[2 + side],
            kind,
        )

    output = restore(output.reshape(grad_out.shape))
    gain_two = jnp.sum(gain_two, axis=0)

    sent = sums_of(1, 1 - core, BF)
    arrived = swap(sent[0], "seq", 1), swap(sent[1], "seq", 1)
    meta = after(core, sent)
    mine = sums_of(0, meta, F32)
    arrived = after(arrived, mine, output)
    twos = [(2**k, 2) for k in range(owners.bit_length() - 1)]
    orders = [twos, twos[1:] + twos[:1]]
    chains = []
    for at in range(2):
        total = (mine[at] + arrived[at].astype(F32)).astype(BF)
        total = total.reshape((2,) * len(twos) + (-1, total.shape[1]))
        chains.append(split_blocks(total, "dp", twos[::-1], orders[at][0]))

    def step_on(at, place, parts, *first):
        total = join_blocks(parts[0], "dp", orders[at][place], *first)
        if place + 1 == len(twos):
            return total
        return split_blocks(total.astype(BF), "dp", parts[1], orders[at][place + 1])

    def to_far(slot):
        found = by_half(grad_attended[slot].reshape(2, 2, ROWS, width)).reshape(4, ROWS, width)
        return found, swap(found[2:], "seq", 2)

    def from_near(found, far):
        got = swap(jnp.stack([found[1], far[1]]), "seq", 1)
        return jnp.stack([found[0], got[0], far[0], got[1]])

    def attend_slot(slot, meta, rows):
        return attend_back(
            meta, sources[slot], rows, pre_back, post_back, probs[slot], weights[slot], FLOPS[slot]
        )

    found, far = to_far(0)
    far = after(far, mine)
    next_found, next_far = to_far(1)
    meta = after(metas[0], chains)
    stay, away, back_pre, back_post = attend_slot(0, meta, from_near(found, far))
    grad_mixes = jnp.stack([back_pre[:, :heads], back_post[:, :heads]])
    chains = [step_on(at, 0, chains[at], stay) for at in range(2)]
    away, next_far = lax.optimization_barrier((away, next_far, chains))[:2]
    next_rows = from_near(next_found, next_far)
    summed = (stay + swap(away, "seq", 1).astype(F32)).astype(BF)
    far = swap(summed[1], "seq", 2)
    meta = after(metas[1], summed, chains)
    stay, away, back_pre, back_post = attend_slot(1, meta, next_rows)
    grad_mixes = grad_mixes + jnp.stack([back_pre[:, :heads], back_post[:, :heads]])
    chains = [step_on(at, 1, chains[at], stay) for at in range(2)]
    away, far = lax.optimization_barrier((away, far, chains))[:2]
    grad_cols = [(summed[0], far)]
    summed = (stay + swap(away, "seq", 1).astype(F32)).astype(BF)
    chains = [(after(parts, summed), left) for parts, left in chains]
    far = swap(summed[1], "seq", 2)

    seqs = [jnp.stack([sequence_of(s, pair), sequence_of(s, 1 - pair)]) for s in range(2)]

    def to_tokens(slot, before):
        return token_grads(
            slot,
            seqs[slot].astype(jnp.int32),
            gain_vals,
            *grad_cols[slot],
            weight_qkv,
            tokens,
            grad_resid,
            before,
        )

    begun = to_tokens(0, None)
    for turn in range(2, len(twos)):
        chains = [step_on(at, turn, chains[at], begun) for at in range(2)]
    first_part, second_part = chains
    others = first_part.astype(BF), second_part.astype(BF)
    far, begun, others = lax.optimization_barrier((far, begun, others))
    grad_cols.append((summed[0], far))
    cols = grad_cols[0] + grad_cols[1]
    sent = first_grads((1 - core)[None], first_in, cols, BF)
    others = after(others, sent)
    qkv_mine = first_grads(after(core, sent)[None], first_in, cols, F32)

    def over_pairs(total):
        total = lax.optimization_barrier(jax.tree.map(lambda v: v.astype(BF), total))
        return jax.tree.map(lambda v: v.astype(F32) + swap(v, "seq", 2).astype(F32), total)

    arrived = after(swap(sent, "seq", 1), qkv_mine)
    qkv_total = (qkv_mine + arrived.astype(F32)).astype(BF)
    grad_rows_tokens, gain_more = to_tokens(1, begun[0])
    gain_one = jnp.sum(begun[1] + gain_more, axis=0)
    qkv_total = qkv_total.reshape((2,) * len(twos) + (own_rows, side))
    third = side // LANES // 3 * LANES
    chains = [qkv_total[..., third:], qkv_total[..., :third]]
    chains = [split_blocks(chains[at], "dp", twos[::-1], orders[at][0]) for at in range(2)]
    others = over_pairs(others)
    small = jnp.concatenate([gain_one, gain_two, grad_mixes.reshape(-1)])
    count = small.shape[0]
    small = jnp.pad(small, (0, -(count + 1) % (8 * LANES) + 1)).reshape(-1, LANES)
    chains = [step_on(at, 0, chains[at]) for at in range(2)]

    first_halves = (others[0], swap(others[0], "seq", 1))
    last_halves = (others[1], swap(others[1], "seq", 1))
    red_proj = by_core(*[g[:, cut - half :] for g in first_halves], 1)
    red_inner = by_core(
        *[g[:, : cut - half].reshape(own_rows, owners, 1, slice_ff) for g in first_halves], 2
    ).reshape(own_rows, hidden)
    red_outer = by_core(*last_halves, 0)
    squares = (
        jnp.sum(red_proj * red_proj)
        + jnp.sum(red_inner * red_inner)
        + jnp.sum(red_outer * red_outer)
    )
    small = small + swap(small, "seq", 1)
    small = small + swap(small, "seq", 2)
    pins = [(), (small,)]
    for turn in range(1, len(twos)):
        pin = pins[turn - 1] if turn <= len(pins) else ()
        chains = [step_on(at, turn, chains[at], *pin) for at in range(2)]
    qkv_total = jnp.concatenate(chains[::-1], axis=-1)
    qkv_total = over_pairs(qkv_total)
    red_qkv = by_core(qkv_total, swap(qkv_total, "seq", 1), 1)

    squares = squares + jnp.sum(red_qkv * red_qkv)
    place = lax.broadcasted_iota(jnp.int32, small.shape, 0) * LANES
    place = place + lax.broadcasted_iota(jnp.int32, small.shape, 1)
    small = sum_everywhere(jnp.where(place == count, squares, small), "dp").reshape(-1)
    gain_all = small[: 2 * width].reshape(2, width)
    red_gains = lax.dynamic_slice_in_dim(gain_all, lax.axis_index("dp") * own_rows, own_rows, 1)
    red_mixes = small[2 * width : count].reshape(mixes.shape)
    grad_norm = jnp.sqrt(
        small[count] + jnp.sum(gain_all * gain_all) + jnp.sum(red_mixes * red_mixes)
    )
    factor = CLIP / jnp.maximum(grad_norm, CLIP)
    clipped_gains = red_gains * factor
    qkv_new = adamw(qkv_weight, qkv_first, qkv_second, qkv_average, red_qkv * factor, 0.03)
    proj_new = adamw(proj_weight, proj_first, proj_second, proj_average, red_proj * factor, 0.1)
    inner_new = adamw(
        inner_weight, inner_first, inner_second, inner_average, red_inner * factor, 0.03
    )
    outer_new = adamw(
        outer_weight, outer_first, outer_second, outer_average, red_outer * factor, 0.02
    )
    gain_new = adamw(gains, gain_first, gain_second, gain_average, clipped_gains, 0.3)
    mix_new = adamw(mixes, mix_first, mix_second, mix_average, red_mixes * factor, 0.3)
    return (
        output,
        grad_rows_tokens,
        grad_norm,
        *qkv_new,
        *proj_new,
        *inner_new,
        *outer_new,
        *gain_new,
        *mix_new,
        clipped_gains,
    )


def solution(mesh):
    rows = P("dp", "seq", None)
    matrix = P("dp", None)
    vector = P(None, "dp")
    in_specs = (rows, rows, P("dp")) + (matrix,) * 16 + (vector,) * 4 + (P(),) * 4
    out_specs = (rows, rows, P()) + (matrix,) * 16 + (vector,) * 4 + (P(),) * 4 + (vector,)
    return jax.shard_map(
        on_device, mesh=mesh, in_specs=in_specs, out_specs=out_specs, check_vma=False
    )
```

time: 754 us -> 564 us (0.75)
  matrix products: 106 us -> 0 us
  Pallas kernels: 125 us -> 216 us
  local copies, waits for them, and re-layouts: 127 us -> 57.7 us
  waiting for transfers between devices: 154 us -> 113 us
  other arithmetic: 97.1 us -> 71.9 us
  starting transfers between devices: 114 us -> 92.3 us
  between operations: 29.8 us -> 15.6 us
    pallas_call x0 -> x10, Pallas kernels: none -> 113 us  [the longest x1 46.2 us: feed_forward(): pl.pallas_call(partial(feed_kernel, offs), grid_spec=pltpu.PrefetchScalar...]
    dot_general x35 -> x0, matrix products: 106 us -> none  [the longest x12 16.4 us: dot(): return lax.dot_general(left, right, dims, preferred_element_type=F32)]
    ppermute x104 -> x63, waiting for transfers between devices: 154 us -> 113 us  [swap(): return lax.ppermute(value, axis, [(i, i ^ mask) for i in range(size)])]
    ppermute x104 -> x63, starting transfers between devices: 114 us -> 92.3 us  [swap(): return lax.ppermute(value, axis, [(i, i ^ mask) for i in range(size)])]
    mul x12 -> x0, local copies, waits for them, and re-layouts: 17.8 us -> none  [the longest x8 14.1 us: spread(): wide = both[:, :, None, :, None] * eye[None, None, :, None, :]]
    dynamic_slice x6 -> x1, local copies, waits for them, and re-layouts: 16.7 us -> 0.09 us  [split_blocks(): lax.dynamic_index_in_dim(blocks, jnp.bitwise_xor(mine, k), place, False)]
    gather x9 -> x0, local copies, waits for them, and re-layouts: 15.1 us -> none  [the longest x5 8.08 us: reduce_shards(): blocks = blocks.at[order].get(mode='promise_in_bounds')]
    pallas_call x2, Pallas kernels: 58 us -> 46.9 us  [attend(): pl.pallas_call(forward_kernel, grid_spec=pltpu.PrefetchScalarGridSpec(num...]
  transfers between devices with their start and end apart: 107 -> 63, of which waited for: 32 -> 19; matrix products, arithmetic and copies ran while one was open for 36% -> 16% of each run, Pallas kernels for 17% -> 26%
where the time goes in v2:
time: 564 us; the launch traced here: 566 us
  Pallas kernels  216 us (38%)
  waiting for transfers between devices  113 us (20%)
  starting transfers between devices  92.3 us (16%)
  other arithmetic  71.9 us (13%)
  local copies, waits for them, and re-layouts  57.7 us (10%)
  between operations  15.6 us (3%)
    ppermute x63, waiting for transfers between devices, swap(): return lax.ppermute(value, axis, [(i, i ^ mask) for i in range(size)])  113 us
    ppermute x63, starting transfers between devices, swap(): return lax.ppermute(value, axis, [(i, i ^ mask) for i in range(size)])  92.3 us
    pallas_call x2, Pallas kernels, attend_back(): pl.pallas_call(backward_kernel, grid_spec=pltpu.PrefetchScalarGridSpec(nu...  55.9 us
    pallas_call x2, Pallas kernels, attend(): pl.pallas_call(forward_kernel, grid_spec=pltpu.PrefetchScalarGridSpec(num...  46.9 us
    pallas_call x1, Pallas kernels, feed_forward(): pl.pallas_call(partial(feed_kernel, offs), grid_spec=pltpu.PrefetchScalar...  46.2 us
    pallas_call x2, Pallas kernels, weight_sums(): pl.pallas_call(weight_kernel, in_specs=[pl.BlockSpec(memory_space=pltpu.S...  26.4 us
    add x6, other arithmetic, adamw(): average_new = EMA_KEEP * average + (1.0 - EMA_KEEP) * weight_new  14.6 us
    pallas_call x2, Pallas kernels, token_grads(): pl.pallas_call(token_grads_kernel, grid_spec=pltpu.PrefetchScalarGridSpec...  13.9 us
  transfers between devices with their start and end apart: 63, of which 19 were waited for; matrix products, arithmetic and copies ran while one was open for 16% of the time, Pallas kernels for 26%

profile of v2, /device:TPU:0, one launch (start us, length us, event | category | flops | bytes accessed | tf_op | source)
XLA Modules:
  0.0 566.4 jit_solution(4387668171300078362)
XLA Ops:
  43.7 10.4 %collective-permute-done.2.refs_2_ = bf16[2,96,1280]{2,1,0:T(8,128)(2,1)S(1)} collective-permute-done((bf16[2,96,1280]{2,1,0:T(8,128)(2,1)S(1)}, bf16[2,96,1280]{2,1,0:T(8,128)(2,1)S(1)}, u32[]{:S(2)}, u32[]{:S(2)}) %collective-permute-start.2) | collective-permute-done | bytes 491552 | tf_op jit(solution)/shard_map/ppermute | solution.py:60
  54.1 8.9 %collective-permute-done.3.refs_3_ = bf16[2,96,1280]{2,1,0:T(8,128)(2,1)} collective-permute-done((bf16[2,96,1280]{2,1,0:T(8,128)(2,1)S(1)}, bf16[2,96,1280]{2,1,0:T(8,128)(2,1)}, u32[]{:S(2)}, u32[]{:S(2)}) %collective-permute-start.3) | collective-permute-done | bytes 491552 | tf_op jit(solution)/shard_map/ppermute | solution.py:60
  65.4 8.4 %collective-permute-done.10 = bf16[1,96,3456]{2,1,0:T(8,128)(2,1)} collective-permute-done((bf16[1,96,3456]{2,1,0:T(8,128)(2,1)}, bf16[1,96,3456]{2,1,0:T(8,128)(2,1)}, u32[]{:S(2)}, u32[]{:S(2)}) %collective-permute-start.10) | collective-permute-done | bytes 663584 | tf_op jit(solution)/shard_map/ppermute | solution.py:60
  81.8 9.0 %first_product.3 = (bf16[1024,2304]{1,0:T(8,128)(2,1)}, bf16[1024,768]{1,0:T(8,128)(2,1)S(1)}, f32[8,768]{1,0:T(8,128)S(1)}, bf16[768,2304]{1,0:T(8,128)(2,1)S(1)}) custom-call(s32[2]{0:T(128)S(1)} %get-tuple-element.124.meta, bf16[1024,768]{1,0:T(8,128)(2,1)S(1)} %bitcast.185, bf16[2,96,1280]{2,1,0:T(8,128)(2,1)S(1)} %pad_maximum_fusion.9.refs_0_, ...), custom_call_target="tpu_custom_call" | custom-call | flops 4000000000 | bytes 5242880 | tf_op jit(solution)/shard_map/first_product/pallas_call | solution.py:769
  98.9 25.5 %collective-permute-done.8.refs_2_ = bf16[256,2304]{1,0:T(8,128)(2,1)S(1)} collective-permute-done((bf16[256,2304]{1,0:T(8,128)(2,1)S(1)}, bf16[256,2304]{1,0:T(8,128)(2,1)S(1)}, u32[]{:S(2)}, u32[]{:S(2)}) %collective-permute-start.8) | collective-permute-done | bytes 1179680 | tf_op jit(solution)/shard_map/ppermute | solution.py:60
  131.7 29.5 %attend.2 = (bf16[4,128,768]{2,1,0:T(8,128)(2,1)}, bf16[5,12,128,1024]{3,2,1,0:T(8,128)(2,1)}, bf16[5,12,128,1024]{3,2,1,0:T(8,128)(2,1)}) custom-call(s32[3]{0:T(128)} %add_add_fusion.1.meta, bf16[256,2304]{1,0:T(8,128)(2,1)} %copy-done.35, bf16[256,2304]{1,0:T(8,128)(2,1)} %copy-done.63, bf16[256,2304]{1,0:T(8,128)(2,1)} %copy-done.64, ...), custom_call_target="tpu_custom_call" | custom-call | flops 60000002048 | bytes 1048576 | tf_op jit(solution)/shard_map/attend/pallas_call | solution.py:426
  165.6 17.3 %attend.3 = (bf16[4,128,768]{2,1,0:T(8,128)(2,1)}, bf16[5,12,128,1024]{3,2,1,0:T(8,128)(2,1)}, bf16[5,12,128,1024]{3,2,1,0:T(8,128)(2,1)}) custom-call(s32[3]{0:T(128)} %add_add_fusion.2.meta, bf16[256,2304]{1,0:T(8,128)(2,1)} %copy-done.12, bf16[256,2304]{1,0:T(8,128)(2,1)} %copy-done.16, bf16[256,2304]{1,0:T(8,128)(2,1)} %copy-done.17, ...), custom_call_target="tpu_custom_call" | custom-call | flops 1000000000 | bytes 1048576 | tf_op jit(solution)/shard_map/attend/pallas_call | solution.py:426
  186.9 8.5 %collective-permute-done.18 = bf16[2,128,768]{2,1,0:T(8,128)(2,1)S(1)} collective-permute-done((bf16[2,128,768]{2,1,0:T(8,128)(2,1)S(1)}, bf16[2,128,768]{2,1,0:T(8,128)(2,1)S(1)}, u32[]{:S(2)}, u32[]{:S(2)}) %collective-permute-start.18) | collective-permute-done | bytes 393248 | tf_op jit(solution)/shard_map/ppermute | solution.py:60
  200.9 46.2 %feed_forward.1 = (bf16[1024,768]{1,0:T(8,128)(2,1)}, f32[1024,768]{1,0:T(8,128)}, bf16[1024,768]{1,0:T(8,128)(2,1)}, bf16[1024,768]{1,0:T(8,128)(2,1)}, f32[8,7...) custom-call(s32[2]{0:T(128)} %copy-done.5, ...), custom_call_target="tpu_custom_call" | custom-call | flops 22000001024 | bytes 40000000 | tf_op jit(solution)/shard_map/feed_forward/pallas_call | solution.py:636
  247.0 12.5 %weight_sums.2 = (bf16[768,1920]{1,0:T(8,128)(2,1)}, bf16[1536,768]{1,0:T(8,128)(2,1)}) custom-call(s32[1]{0:T(128)} %bitcast.44.meta, bf16[1024,768]{1,0:T(8,128)(2,1)} %get-tuple-element.148.second_in, bf16[1024,768]{1,0:T(8,128)(2,1)} %bitcast.204, bf16[1024,768]{1,0:T(8,128)(2,1)} %get-tuple-element.149.resid_low, ...), custom_call_target="tpu_custom_call" | custom-call | flops 6000000000 | bytes 20000000 | tf_op jit(solution)/shard_map/weight_sums/pallas_call | solution.py:690
  262.2 14.0 %weight_sums.3 = (f32[768,1920]{1,0:T(8,128)}, f32[1536,768]{1,0:T(8,128)}) custom-call(s32[1]{0:T(128)} %bitcast.45.meta, bf16[1024,768]{1,0:T(8,128)(2,1)} %get-tuple-element.148.second_in, bf16[1024,768]{1,0:T(8,128)(2,1)} %bitcast.205, bf16[1024,768]{1,0:T(8,128)(2,1)} %get-tuple-element.149.resid_low, bf16[1024,768]{1,0:T(8,128)(2,1)} %bitcast_select_fusion.grad_out, ...), custom_call_target="tpu_custom_call" | custom-call | flops 6000000000 | bytes 20000000 | tf_op jit(solution)/shard_map/weight_sums/pallas_call | solution.py:690
  292.9 11.7 %collective-permute-start.30 = (bf16[2,2,96,1920]{3,2,1,0:T(8,128)(2,1)}, bf16[2,2,96,1920]{3,2,1,0:T(8,128)(2,1)}, u32[]{:S(2)}, u32[]{:S(2)}) collective-permute-start(bf16[2,2,96,1920]{3,2,1,0:T(8,128)(2,1)} %get-tuple-element.300), channel_id=1, source_target_pairs={{0,4},{4,0},{8,12},{12,8},{16,20},{20,16},{24,28},{28,24},{1,5},{5... | collective-permute-start | bytes 4423688 | tf_op jit(solution)/shard_map/ppermute | solution.py:60
  304.6 41.2 %attend_back.2 = (f32[2,2304,256]{2,1,0:T(8,128)}, bf16[2,2304,256]{2,1,0:T(8,128)(2,1)}, f32[12,128]{1,0:T(8,128)}, f32[12,128]{1,0:T(8,128)}) custom-call(s32[3]{0:T(128)} %add_add_fusion.1.meta, bf16[256,2304]{1,0:T(8,128)(2,1)} %copy-done.35, bf16[256,2304]{1,0:T(8,128)(2,1)} %copy-done.63, bf16[256,2304]{1,0:T(8,128)(2,1)} %copy-done.64, ...), custom_call_target="tpu_custom_call" | custom-call | flops 60000002048 | bytes 1048576 | tf_op jit(solution)/shard_map/attend_back/pallas_call | solution.py:472
  360.4 14.7 %attend_back.3 = (f32[2,2304,256]{2,1,0:T(8,128)}, bf16[2,2304,256]{2,1,0:T(8,128)(2,1)}, f32[12,128]{1,0:T(8,128)}, f32[12,128]{1,0:T(8,128)}) custom-call(s32[3]{0:T(128)} %add_add_fusion.2.meta, bf16[256,2304]{1,0:T(8,128)(2,1)} %copy-done.12, bf16[256,2304]{1,0:T(8,128)(2,1)} %copy-done.16, bf16[256,2304]{1,0:T(8,128)(2,1)} %copy-done.17, ...), custom_call_target="tpu_custom_call" | custom-call | flops 1000000000 | bytes 1048576 | tf_op jit(solution)/shard_map/attend_back/pallas_call | solution.py:472
  375.1 8.4 %collective-permute-done.36 = bf16[2,192,768]{2,1,0:T(8,128)(2,1)} collective-permute-done((bf16[2,192,768]{2,1,0:T(8,128)(2,1)}, bf16[2,192,768]{2,1,0:T(8,128)(2,1)}, u32[]{:S(2)}, u32[]{:S(2)}) %collective-permute-start.36) | collective-permute-done | bytes 589856 | tf_op jit(solution)/shard_map/ppermute | solution.py:60
  399.9 17.9 %collective-permute-start.40 = (bf16[192,768]{1,0:T(8,128)(2,1)}, bf16[192,768]{1,0:T(8,128)(2,1)S(1)}, u32[]{:S(2)}, u32[]{:S(2)}) collective-permute-start(bf16[192,768]{1,0:T(8,128)(2,1)} %get-tuple-element.191), channel_id=1, source_target_pairs={{0,4},{4,0},{8,12},{12,8},{16,20},{20,16},{24,28},{28,24},{1,5},{5... | collective-permute-start | bytes 884744 | tf_op jit(solution)/shard_map/ppermute | solution.py:60
  419.1 6.4 %token_grads.2 = (f32[4,256,768]{2,1,0:T(8,128)}, f32[8,768]{1,0:T(8,128)S(1)}) custom-call(s32[2]{0:T(128)S(1)} %pad_add_fusion.3.meta, f32[8,768]{1,0:T(8,128)S(1)} %get-tuple-element.125.gains, bf16[2304,256]{1,0:T(8,128)(2,1)S(1)} %get-tuple-element.302.near.refs_0_, bf16[2304,256]{1,0:T(8,128)(2,1)S(1)} %copy-done.7, bf16[768,2304]{1,0:T(8,128)(2,1)} %copy-done.10, ...), custom_call_target="tpu_custom_call" | custom-call | flops 4000000000 | bytes 5242880 | tf_op jit(solution)/shard_map/token_grads/pallas_call | solution.py:842
  435.9 7.4 %token_grads.3 = (f32[4,256,768]{2,1,0:T(8,128)}, f32[8,768]{1,0:T(8,128)S(1)}) custom-call(s32[2]{0:T(128)S(1)} %get-tuple-element.363.meta, f32[8,768]{1,0:T(8,128)S(1)} %get-tuple-element.125.gains, bf16[2304,256]{1,0:T(8,128)(2,1)S(1)} %copy-done.3, bf16[2304,256]{1,0:T(8,128)(2,1)} %collective-permute-done.38.far.refs_3_, ...), custom_call_target="tpu_custom_call", output_to_operand_aliasing={{0}: (7, {})} | custom-call | flops 4000000000 | bytes 5242880 | tf_op jit(solution)/shard_map/token_grads/pallas_call | solution.py:842
  445.9 5.8 %first_grads.3 = f32[768,1152]{1,0:T(8,128)} custom-call(s32[1]{0:T(128)} %bitcast.71.meta, bf16[1024,768]{1,0:T(8,128)(2,1)} %copy-done.11, bf16[2304,256]{1,0:T(8,128)(2,1)S(1)} %get-tuple-element.302.near.refs_0_, bf16[2304,256]{1,0:T(8,128)(2,1)S(1)} %copy-done.9, bf16[2304,256]{1,0:T(8,128)(2,1)S(1)} %copy-done.4, ...), custom_call_target="tpu_custom_call" | custom-call | flops 3000000000 | bytes 5242880 | tf_op jit(solution)/shard_map/first_grads/pallas_call | solution.py:801
  455.4 15.5 %collective-permute-start.51 = (bf16[2,2,96,768]{3,2,0,1:T(8,128)(2,1)S(1)}, bf16[2,2,96,768]{3,2,0,1:T(8,128)(2,1)S(1)}, u32[]{:S(2)}, u32[]{:S(2)}) collective-permute-start(bf16[2,2,96,768]{3,2,0,1:T(8,128)(2,1)S(1)} %bitcast.212), channel_id=1, source_target_pairs={{0,4},{4,0},{8,12},{12,8},{16,20},{20,16},{24,28},{28,24},{1,5},{5... | collective-permute-start | bytes 1769480 | tf_op jit(solution)/shard_map/ppermute | solution.py:60
  471.1 8.7 %collective-permute-done.47 = bf16[2,96,384]{2,1,0:T(8,128)(2,1)S(1)} collective-permute-done((bf16[2,96,384]{2,1,0:T(8,128)(2,1)S(1)}, bf16[2,96,384]{2,1,0:T(8,128)(2,1)S(1)}, u32[]{:S(2)}, u32[]{:S(2)}) %collective-permute-start.47) | collective-permute-done | bytes 147488 | tf_op jit(solution)/shard_map/ppermute | solution.py:60
  479.9 6.2 %collective-permute-start.48 = (bf16[96,384]{1,0:T(8,128)(2,1)S(1)}, bf16[96,384]{1,0:T(8,128)(2,1)S(1)}, u32[]{:S(2)}, u32[]{:S(2)}) collective-permute-start(bf16[96,384]{1,0:T(8,128)(2,1)S(1)} %dynamic-slice_bitcast_fusion.18), channel_id=1, source_target_pairs={{0,4},{4,0},{8,12},{12,8},{16,20},{20,16},{24,28},{28,24},{1,5},{5... | collective-permute-start | bytes 221192 | tf_op jit(solution)/shard_map/ppermute | solution.py:60
  488.4 6.2 %collective-permute-done.52 = bf16[2,96,768]{2,1,0:T(8,128)(2,1)S(1)} collective-permute-done((bf16[2,96,768]{2,1,0:T(8,128)(2,1)S(1)}, bf16[2,96,768]{2,1,0:T(8,128)(2,1)S(1)}, u32[]{:S(2)}, u32[]{:S(2)}) %collective-permute-start.52) | collective-permute-done | bytes 294944 | tf_op jit(solution)/shard_map/ppermute | solution.py:60
  494.8 8.2 %collective-permute-done.53 = bf16[96,768]{1,0:T(8,128)(2,1)S(1)} collective-permute-done((bf16[96,768]{1,0:T(8,128)(2,1)S(1)}, bf16[96,768]{1,0:T(8,128)(2,1)S(1)}, u32[]{:S(2)}, u32[]{:S(2)}) %collective-permute-start.53) | collective-permute-done | bytes 147488 | tf_op jit(solution)/shard_map/ppermute | solution.py:60
  (414 shorter events, 202.2 us)
Async XLA Ops:
  42.9 31.0 %collective-permute-start.10 = (bf16[1,96,3456]{2,1,0:T(8,128)(2,1)}, bf16[1,96,3456]{2,1,0:T(8,128)(2,1)}, u32[]{:S(2)}, u32[]{:S(2)}) collective-permute-start(bf16[1,96,3456]{2,1,0:T(8,128)(2,1)} %maximum_bitcast_fusion.4), channel_id=1, source_target_pairs={{0,16},{4,20},{8,24},{12,28},{16,0},{20,4},{24,8},{28,12},{1,17},{... | collective-permute-start | bytes 1990664 | tf_op jit(solution)/shard_map/ppermute | solution.py:60
  43.2 30.6 %collective-permute-start.4 = (bf16[2,96,1280]{2,1,0:T(8,128)(2,1)S(1)}, bf16[2,96,1280]{2,1,0:T(8,128)(2,1)}, u32[]{:S(2)}, u32[]{:S(2)}) collective-permute-start(bf16[2,96,1280]{2,1,0:T(8,128)(2,1)S(1)} %pad_maximum_fusion.9.refs_0_), channel_id=1, source_target_pairs={{0,1},{1,0},{2,3},{3,2},{4,5},{5,4},{6,7},{7,6},{8,9},{9,8},{10,11... | collective-permute-start | bytes 1474568 | tf_op jit(solution)/shard_map/ppermute | solution.py:60
  43.2 30.6 %collective-permute-start.5 = (bf16[2,96,1280]{2,1,0:T(8,128)(2,1)S(1)}, bf16[2,96,1280]{2,1,0:T(8,128)(2,1)}, u32[]{:S(2)}, u32[]{:S(2)}) collective-permute-start(bf16[2,96,1280]{2,1,0:T(8,128)(2,1)S(1)} %collective-permute-done.1.refs_1_), channel_id=1, source_target_pairs={{0,1},{1,0},{2,3},{3,2},{4,5},{5,4},{6,7},{7,6},{8,9},{9,8},{10,11... | collective-permute-start | bytes 1474568 | tf_op jit(solution)/shard_map/ppermute | solution.py:60
  80.3 44.1 %collective-permute-start.11 = (bf16[2,96,3456]{2,1,0:T(8,128)(2,1)}, bf16[2,96,3456]{2,1,0:T(8,128)(2,1)}, u32[]{:S(2)}, u32[]{:S(2)}) collective-permute-start(bf16[2,96,3456]{2,1,0:T(8,128)(2,1)} %pad_maximum_fusion.3.refs_0_), channel_id=1, source_target_pairs={{0,8},{4,12},{8,0},{12,4},{16,24},{20,28},{24,16},{28,20},{1,9},{5... | collective-permute-start | bytes 3981320 | tf_op jit(solution)/shard_map/ppermute | solution.py:60
  80.3 44.1 %collective-permute-start.12 = (bf16[2,96,3456]{2,1,0:T(8,128)(2,1)}, bf16[2,96,3456]{2,1,0:T(8,128)(2,1)}, u32[]{:S(2)}, u32[]{:S(2)}) collective-permute-start(bf16[2,96,3456]{2,1,0:T(8,128)(2,1)} %pad_maximum_fusion.3.refs_0_), channel_id=1, source_target_pairs={{0,4},{4,0},{8,12},{12,8},{16,20},{20,16},{24,28},{28,24},{1,5},{5... | collective-permute-start | bytes 3981320 | tf_op jit(solution)/shard_map/ppermute | solution.py:60
  96.0 28.4 %collective-permute-start.8 = (bf16[256,2304]{1,0:T(8,128)(2,1)S(1)}, bf16[256,2304]{1,0:T(8,128)(2,1)S(1)}, u32[]{:S(2)}, u32[]{:S(2)}) collective-permute-start(bf16[256,2304]{1,0:T(8,128)(2,1)S(1)} %get-tuple-element.123), channel_id=1, source_target_pairs={{0,2},{1,3},{2,0},{3,1},{4,6},{5,7},{6,4},{7,5},{8,10},{9,11},{10,... | collective-permute-start | bytes 3538952 | tf_op jit(solution)/shard_map/ppermute | solution.py:60
  128.5 36.5 %collective-permute-start.20 = (bf16[2,96,3456]{2,1,0:T(8,128)(2,1)}, bf16[2,96,3456]{2,1,0:T(8,128)(2,1)}, u32[]{:S(2)}, u32[]{:S(2)}) collective-permute-start(bf16[2,96,3456]{2,1,0:T(8,128)(2,1)} %collective-permute-done.11.refs_1_), channel_id=1, source_target_pairs={{0,4},{4,0},{8,12},{12,8},{16,20},{20,16},{24,28},{28,24},{1,5},{5... | collective-permute-start | bytes 3981320 | tf_op jit(solution)/shard_map/ppermute | solution.py:60
  129.1 32.2 %collective-permute-start.15 = (bf16[256,2304]{1,0:T(8,128)(2,1)S(1)}, bf16[256,2304]{1,0:T(8,128)(2,1)S(1)}, u32[]{:S(2)}, u32[]{:S(2)}) collective-permute-start(bf16[256,2304]{1,0:T(8,128)(2,1)S(1)} %get-tuple-element.135.refs_0_), channel_id=1, source_target_pairs={{0,1},{1,0},{2,3},{3,2},{4,5},{5,4},{6,7},{7,6},{8,9},{9,8},{10,11... | collective-permute-start | bytes 3538952 | tf_op jit(solution)/shard_map/ppermute | solution.py:60
  129.1 32.1 %collective-permute-start.14 = (bf16[256,2304]{1,0:T(8,128)(2,1)}, bf16[256,2304]{1,0:T(8,128)(2,1)S(1)}, u32[]{:S(2)}, u32[]{:S(2)}) collective-permute-start(bf16[256,2304]{1,0:T(8,128)(2,1)} %get-tuple-element.134), channel_id=1, source_target_pairs={{0,2},{1,3},{2,0},{3,1},{4,6},{5,7},{6,4},{7,5},{8,10},{9,11},{10,... | collective-permute-start | bytes 3538952 | tf_op jit(solution)/shard_map/ppermute | solution.py:60
  164.5 34.1 %collective-permute-start.21 = (bf16[2,96,3456]{2,1,0:T(8,128)(2,1)}, bf16[2,96,3456]{2,1,0:T(8,128)(2,1)}, u32[]{:S(2)}, u32[]{:S(2)}) collective-permute-start(bf16[2,96,3456]{2,1,0:T(8,128)(2,1)} %pad_maximum_fusion.3.refs_0_), channel_id=1, source_target_pairs={{0,1},{1,0},{2,3},{3,2},{4,5},{5,4},{6,7},{7,6},{8,9},{9,8},{10,11... | collective-permute-start | bytes 3981320 | tf_op jit(solution)/shard_map/ppermute | solution.py:60
  164.7 33.9 %collective-permute-start.22 = (bf16[2,96,3456]{2,1,0:T(8,128)(2,1)}, bf16[2,96,3456]{2,1,0:T(8,128)(2,1)}, u32[]{:S(2)}, u32[]{:S(2)}) collective-permute-start(bf16[2,96,3456]{2,1,0:T(8,128)(2,1)} %collective-permute-done.11.refs_1_), channel_id=1, source_target_pairs={{0,1},{1,0},{2,3},{3,2},{4,5},{5,4},{6,7},{7,6},{8,9},{9,8},{10,11... | collective-permute-start | bytes 3981320 | tf_op jit(solution)/shard_map/ppermute | solution.py:60
  165.1 33.6 %collective-permute-start.23 = (bf16[2,96,3456]{2,1,0:T(8,128)(2,1)}, bf16[2,96,3456]{2,1,0:T(8,128)(2,1)}, u32[]{:S(2)}, u32[]{:S(2)}) collective-permute-start(bf16[2,96,3456]{2,1,0:T(8,128)(2,1)} %collective-permute-done.12.refs_2_), channel_id=1, source_target_pairs={{0,1},{1,0},{2,3},{3,2},{4,5},{5,4},{6,7},{7,6},{8,9},{9,8},{10,11... | collective-permute-start | bytes 3981320 | tf_op jit(solution)/shard_map/ppermute | solution.py:60
  165.2 33.4 %collective-permute-start.24 = (bf16[2,96,3456]{2,1,0:T(8,128)(2,1)}, bf16[2,96,3456]{2,1,0:T(8,128)(2,1)}, u32[]{:S(2)}, u32[]{:S(2)}) collective-permute-start(bf16[2,96,3456]{2,1,0:T(8,128)(2,1)} %collective-permute-done.20.refs_3_), channel_id=1, source_target_pairs={{0,1},{1,0},{2,3},{3,2},{4,5},{5,4},{6,7},{7,6},{8,9},{9,8},{10,11... | collective-permute-start | bytes 3981320 | tf_op jit(solution)/shard_map/ppermute | solution.py:60
  278.1 73.4 %collective-permute-start.29 = (bf16[2,128,768]{2,1,0:T(8,128)(2,1)}, bf16[2,128,768]{2,1,0:T(8,128)(2,1)}, u32[]{:S(2)}, u32[]{:S(2)}) collective-permute-start(bf16[2,128,768]{2,1,0:T(8,128)(2,1)} %slice_bitcast_fusion.4), channel_id=1, source_target_pairs={{0,2},{1,3},{2,0},{3,1},{4,6},{5,7},{6,4},{7,5},{8,10},{9,11},{10,... | collective-permute-start | bytes 1179656 | tf_op jit(solution)/shard_map/ppermute | solution.py:60
  289.4 56.4 %collective-permute-start.31 = (bf16[2,2,192,768]{3,2,1,0:T(8,128)(2,1)}, bf16[2,2,192,768]{3,2,1,0:T(8,128)(2,1)}, u32[]{:S(2)}, u32[]{:S(2)}) collective-permute-start(bf16[2,2,192,768]{3,2,1,0:T(8,128)(2,1)} %get-tuple-element.306), channel_id=1, source_target_pairs={{0,8},{4,12},{8,0},{12,4},{16,24},{20,28},{24,16},{28,20},{1,9},{5... | collective-permute-start | bytes 3538952 | tf_op jit(solution)/shard_map/ppermute | solution.py:60
  292.9 55.4 %collective-permute-start.30 = (bf16[2,2,96,1920]{3,2,1,0:T(8,128)(2,1)}, bf16[2,2,96,1920]{3,2,1,0:T(8,128)(2,1)}, u32[]{:S(2)}, u32[]{:S(2)}) collective-permute-start(bf16[2,2,96,1920]{3,2,1,0:T(8,128)(2,1)} %get-tuple-element.300), channel_id=1, source_target_pairs={{0,4},{4,0},{8,12},{12,8},{16,20},{20,16},{24,28},{28,24},{1,5},{5... | collective-permute-start | bytes 4423688 | tf_op jit(solution)/shard_map/ppermute | solution.py:60
  354.2 29.3 %collective-permute-start.36 = (bf16[2,192,768]{2,1,0:T(8,128)(2,1)}, bf16[2,192,768]{2,1,0:T(8,128)(2,1)}, u32[]{:S(2)}, u32[]{:S(2)}) collective-permute-start(bf16[2,192,768]{2,1,0:T(8,128)(2,1)} %get-tuple-element.322), channel_id=1, source_target_pairs={{0,16},{4,20},{8,24},{12,28},{16,0},{20,4},{24,8},{28,12},{1,17},{... | collective-permute-start | bytes 1769480 | tf_op jit(solution)/shard_map/ppermute | solution.py:60
  354.2 31.8 %collective-permute-start.35 = (bf16[2,96,1920]{2,1,0:T(8,128)(2,1)}, bf16[2,96,1920]{2,1,0:T(8,128)(2,1)}, u32[]{:S(2)}, u32[]{:S(2)}) collective-permute-start(bf16[2,96,1920]{2,1,0:T(8,128)(2,1)} %get-tuple-element.318), channel_id=1, source_target_pairs={{0,8},{4,12},{8,0},{12,4},{16,24},{20,28},{24,16},{28,20},{1,9},{5... | collective-permute-start | bytes 2211848 | tf_op jit(solution)/shard_map/ppermute | solution.py:60
  360.4 30.2 %collective-permute-start.34 = (bf16[2304,256]{1,0:T(8,128)(2,1)}, bf16[2304,256]{1,0:T(8,128)(2,1)S(1)}, u32[]{:S(2)}, u32[]{:S(2)}) collective-permute-start(bf16[2304,256]{1,0:T(8,128)(2,1)} %get-tuple-element.303), channel_id=1, source_target_pairs={{0,2},{1,3},{2,0},{3,1},{4,6},{5,7},{6,4},{7,5},{8,10},{9,11},{10,... | collective-permute-start | bytes 3538952 | tf_op jit(solution)/shard_map/ppermute | solution.py:60
  398.6 30.5 %collective-permute-start.38 = (bf16[2304,256]{1,0:T(8,128)(2,1)}, bf16[2304,256]{1,0:T(8,128)(2,1)}, u32[]{:S(2)}, u32[]{:S(2)}) collective-permute-start(bf16[2304,256]{1,0:T(8,128)(2,1)} %get-tuple-element.304), channel_id=1, source_target_pairs={{0,2},{1,3},{2,0},{3,1},{4,6},{5,7},{6,4},{7,5},{8,10},{9,11},{10,... | collective-permute-start | bytes 3538952 | tf_op jit(solution)/shard_map/ppermute | solution.py:60
  443.9 61.3 %collective-permute-start.43 = (bf16[192,768]{1,0:T(8,128)(2,1)S(1)}, bf16[192,768]{1,0:T(8,128)(2,1)S(1)}, u32[]{:S(2)}, u32[]{:S(2)}) collective-permute-start(bf16[192,768]{1,0:T(8,128)(2,1)S(1)} %copy-done.36), channel_id=1, source_target_pairs={{0,2},{1,3},{2,0},{3,1},{4,6},{5,7},{6,4},{7,5},{8,10},{9,11},{10,... | collective-permute-start | bytes 884744 | tf_op jit(solution)/shard_map/ppermute | solution.py:60
  444.2 42.2 %collective-permute-start.41 = (bf16[96,1920]{1,0:T(8,128)(2,1)S(1)}, bf16[96,1920]{1,0:T(8,128)(2,1)S(1)}, u32[]{:S(2)}, u32[]{:S(2)}) collective-permute-start(bf16[96,1920]{1,0:T(8,128)(2,1)S(1)} %add_convert_fusion.9), channel_id=1, source_target_pairs={{0,2},{1,3},{2,0},{3,1},{4,6},{5,7},{6,4},{7,5},{8,10},{9,11},{10,... | collective-permute-start | bytes 1105928 | tf_op jit(solution)/shard_map/ppermute | solution.py:60
  455.4 30.7 %collective-permute-start.51 = (bf16[2,2,96,768]{3,2,0,1:T(8,128)(2,1)S(1)}, bf16[2,2,96,768]{3,2,0,1:T(8,128)(2,1)S(1)}, u32[]{:S(2)}, u32[]{:S(2)}) collective-permute-start(bf16[2,2,96,768]{3,2,0,1:T(8,128)(2,1)S(1)} %bitcast.212), channel_id=1, source_target_pairs={{0,4},{4,0},{8,12},{12,8},{16,20},{20,16},{24,28},{28,24},{1,5},{5... | collective-permute-start | bytes 1769480 | tf_op jit(solution)/shard_map/ppermute | solution.py:60
  486.5 26.4 %collective-permute-start.42 = (f32[96,1920]{1,0:T(8,128)S(1)}, f32[96,1920]{1,0:T(8,128)}, u32[]{:S(2)}, u32[]{:S(2)}) collective-permute-start(f32[96,1920]{1,0:T(8,128)S(1)} %convert_add_fusion.1), channel_id=1, source_target_pairs={{0,1},{1,0},{2,3},{3,2},{4,5},{5,4},{6,7},{7,6},{8,9},{9,8},{10,11... | collective-permute-start | bytes 2211848 | tf_op jit(solution)/shard_map/ppermute | solution.py:60
  (109 other events, 1080.1 us)
